TPU v7x, 256 devices: a whole 4x4x8 slice. The times are simulated.
256 devices in a mesh: particle: 32 (over z, x_lo, core), slab: 8 (over x_hi, y).
Axes of the slice: x: 4 (x_hi: 2, x_lo: 2; x = x_hi * 2 + x_lo), y: 4, z: 8, core: 2. Of those that a mesh axis runs over, the one named last changes fastest.
Arguments:
- ref_map: bfloat16 [1024, 256], P('slab'), may hold values from -6 to 6
- images: bfloat16 [512, 2, 2048], P(('particle', 'slab')), may hold values from -6 to 6
- ctf_table: bfloat16 [64, 2048], replicated, may hold values from -1 to 1
- ctf_class: int32 [512], P(('particle', 'slab')), may hold values from 0 to 63
- block_index: int32 [512, 64, 16, 4], P(('particle', 'slab')), may hold values from 0 to 1023
- interp_kind: int32 [512, 64, 16, 4], P(('particle', 'slab')), may hold values from 0 to 7
- interp_bank: bfloat16 [8, 128, 128], replicated, may hold values from -0.25 to 0.25
Outputs:
- data_map: float32 [1024, 256], P(('particle', 'slab'))
- weight_map: float32 [1024, 128], P(('particle', 'slab'))
- posterior: float32 [512, 64], P(('particle', 'slab'))
Inputs may be any that keep to these rules, and one draw needn't show every extreme that they name: `block_index`: map blocks of the whole window. `interp_kind`: bank entries. `ctf_class`: rows of ctf_table.
All inputs are finite; a program needn't handle non-finite values.
Results may differ from a plain program's by a relative error of at most 0.0013.
Values may be sent and summed in bfloat16 or wider, within the bound.
A program may use at most 128 MiB of HBM per device.

v0:
```python
import jax
import jax.numpy as jnp
from jax import lax
from jax.sharding import PartitionSpec as P

LINE = 256
PLINES = 8
SIDE = 32


def shift_table(pix_total):
    pixels = jnp.arange(pix_total, dtype=jnp.int32)
    freq_x = pixels % LINE - LINE // 2
    freq_y = pixels // LINE - PLINES // 2
    shift_ids = jnp.arange(SIDE * SIDE, dtype=jnp.int32)
    shift_x = shift_ids % SIDE - SIDE // 2
    shift_y = shift_ids // SIDE - SIDE // 2
    phase_num = (freq_x[:, None] * shift_x[None, :] + freq_y[:, None] * shift_y[None, :]) % LINE
    angles = 2.0 * jnp.pi / LINE * phase_num.astype(jnp.float32)
    return jnp.concatenate([jnp.cos(angles), -jnp.sin(angles)], axis=0).astype(jnp.bfloat16)


def score_group(table_rows, shifts, images, ctf_gain, block_index, interp_kind, block_total):
    image_count, cand_count, block_count, tap_count = block_index.shape
    blk_width = table_rows.shape[1] // 2
    row_ids = interp_kind * block_total + block_index
    picked = jnp.take(table_rows, row_ids.reshape(-1), axis=0)
    picked = picked.reshape(image_count, cand_count, block_count, tap_count, 2, blk_width)
    projection = jnp.sum(picked.astype(jnp.float32), axis=3)
    image_pix = images.astype(jnp.float32).reshape(image_count, 2, block_count, blk_width)
    real_part = image_pix[:, 0][:, None]
    imag_part = image_pix[:, 1][:, None]
    ctf_grid = ctf_gain.reshape(image_count, 1, block_count, blk_width)
    proj_re = projection[:, :, :, 0, :]
    proj_im = projection[:, :, :, 1, :]
    cross_re = ctf_grid * (real_part * proj_re + imag_part * proj_im)
    cross_im = ctf_grid * (imag_part * proj_re - real_part * proj_im)
    stacked = jnp.concatenate(
        [
            cross_re.reshape(image_count, cand_count, -1),
            cross_im.reshape(image_count, cand_count, -1),
        ],
        axis=-1,
    ).astype(jnp.bfloat16)
    scores = jnp.dot(
        stacked.reshape(image_count * cand_count, -1), shifts, preferred_element_type=jnp.float32
    )
    energy = jnp.mean(scores * scores, axis=-1).reshape(image_count, cand_count)
    posterior = cand_count * energy / (jnp.sum(energy, axis=1, keepdims=True) + 1e-06)
    contrib = jnp.stack([ctf_grid * real_part, ctf_grid * imag_part, ctf_grid * ctf_grid], axis=-2)
    contrib = posterior[:, :, None, None, None] * contrib
    rows_all = jnp.broadcast_to(
        contrib[:, :, :, None], (image_count, cand_count, block_count, tap_count, 3, blk_width)
    )
    seg_sums = jax.ops.segment_sum(
        rows_all.reshape(-1, 3 * blk_width), row_ids.reshape(-1), num_segments=table_rows.shape[0]
    )
    return (posterior, seg_sums)


def local(ref_map, images, ctf_table, ctf_class, block_index, interp_kind, interp_bank):
    kind_count = interp_bank.shape[0]
    blk_width = interp_bank.shape[1]
    slab_piece = lax.all_gather(ref_map, "slab", axis=0, tiled=True)
    blocks = slab_piece.reshape(slab_piece.shape[0], 2, blk_width)
    transformed = jnp.einsum(
        "rcv,kvq->krcq", blocks, interp_bank, preferred_element_type=jnp.float32
    ).astype(jnp.bfloat16)
    block_total = transformed.shape[1]
    table_rows = transformed.reshape(kind_count * block_total, 2 * blk_width)
    onehot = (
        ctf_class[:, None] == jnp.arange(ctf_table.shape[0], dtype=jnp.int32)[None, :]
    ).astype(jnp.bfloat16)
    ctf_gain = jnp.dot(onehot, ctf_table, preferred_element_type=jnp.float32)
    posterior, seg_sums = score_group(
        table_rows,
        shift_table(images.shape[2]),
        images,
        ctf_gain,
        block_index,
        interp_kind,
        block_total,
    )
    share_rows = block_total // (lax.axis_size("particle") * lax.axis_size("slab"))
    bank_full = interp_bank.astype(jnp.float32)
    seg_grid = seg_sums.reshape(kind_count, block_total, 3, blk_width)
    summed = jnp.einsum("kvcq,kwq->vcw", seg_grid, bank_full, precision=lax.Precision.HIGHEST)
    merged = lax.psum_scatter(
        summed.reshape(lax.axis_size(("particle", "slab")) * share_rows, 3 * blk_width),
        ("particle", "slab"),
        scatter_dimension=0,
        tiled=True,
    )
    data_map = merged[:, : 2 * blk_width]
    weight_map = merged[:, 2 * blk_width :]
    return (data_map, weight_map, posterior)


def solution(mesh):
    in_specs = (
        P("slab", None),
        P(("particle", "slab"), None, None),
        P(),
        P(("particle", "slab")),
        P(("particle", "slab"), None, None, None),
        P(("particle", "slab"), None, None, None),
        P(),
    )
    out_specs = (
        P(("particle", "slab"), None),
        P(("particle", "slab"), None),
        P(("particle", "slab"), None),
    )
    return jax.shard_map(local, mesh=mesh, in_specs=in_specs, out_specs=out_specs, check_vma=False)
```

profile of v0, /device:TPU:2, one launch (start us, length us, event | category | flops | bytes accessed | tf_op | source)
XLA Modules:
  0.0 556.7 jit_solution(9398785621788362718)
XLA Ops:
  7.2 0.0 copy-start
  7.2 0.0 all-reduce.3.cloned.1.call-start
  7.2 0.9 compare_and_fusion
  8.2 0.5 copy.43
  8.7 0.7 broadcast_in_dim_reshape.3
  9.5 0.6 reshape.217
  10.1 0.7 reshape.206
  10.9 1.0 copy.46
  11.9 30.7 %all_gather.3 = bf16[1024,256]{0,1:T(8,128)(2,1)S(1)} all-gather(bf16[128,256]{0,1:T(8,128)(2,1)S(1)} %copy.46), channel_id=1, replica_groups=mesh['particle'=32,'slab'=8] {'slab'}, dimensions={0}, use_global_device_ids=true | all-gather | bytes 589824 | tf_op jit(solution)/shard_map/all_gather | solution.py:64
  42.6 1.1 copy.55
  43.7 4.2 convert_bitcast_fusion
  47.9 11.1 %copy.63 = bf16[8,1024,2,128]{3,2,1,0:T(2,128)(2,1)} copy(bf16[8,1024,2,128]{1,3,2,0:T(8,128)(2,1)} %convert_bitcast_fusion) | data formatting | bytes 8388608 | tf_op jit(solution)/shard_map/reshape | solution.py:70
  59.1 4.7 copy.90
  63.8 33.6 %gather_fusion = bf16[8192,256]{1,0:T(8,128)(2,1)} fusion(bf16[8192,256]{1,0:T(8,128)(2,1)} %bitcast.114, s32[8192]{0:T(1024)S(1)} %broadcast_clamp_fusion), kind=kCustom, calls=%fused_computation | custom fusion | bytes 8421376 | tf_op jit(solution)/shard_map/jit(_take)/gather | solution.py:27
  97.4 0.0 copy-start.3
  97.4 6.9 %gather.7 = bf16[2,64,16,4,2,128]{5,4,3,2,1,0:T(2,128)(2,1)} reshape(bf16[8192,256]{1,0:T(8,128)(2,1)} %gather_fusion) | data formatting | bytes 8388608 | tf_op jit(solution)/shard_map/jit(_take)/gather | solution.py:27
  104.3 0.6 copy.45
  104.9 14.8 %convert_reduce_fusion = f32[2,64,16,2,128]{4,3,2,1,0:T(2,128)S(1)} fusion(bf16[2,64,16,4,2,128]{5,4,3,2,1,0:T(2,128)(2,1)} %gather.7, pred[2,64,16,4]{3,2,1,0:T(8,128)(4,1)S(1)} %copy.45), kind=kLoop, calls=%fused_computation.17 | loop fusion | flops 5767168 | bytes 6299648 | tf_op jit(solution)/shard_map/reduce_sum | solution.py:29
  119.8 5.8 %slice_reduce_fusion.1 = (f32[2,64,16,128]{3,2,1,0:T(8,128)S(1)}, f32[2,64,16,128]{3,2,1,0:T(8,128)S(1)}) fusion(f32[2,64,16,2,128]{4,3,2,1,0:T(2,128)S(1)} %convert_reduce_fusion), kind=kLoop, calls=%fused_computation.36 | loop fusion | bytes 4194304 | tf_op jit(solution)/shard_map/slice | solution.py:34
  125.5 0.0 copy-done
  125.5 0.0 copy-done.3
  125.5 0.2 fusion.43
  125.8 1.0 fusion.17
  126.8 48.6 %cosine_convert_fusion = (bf16[2048,1024]{1,0:T(8,128)(2,1)S(1)}, bf16[2048,1024]{1,0:T(8,128)(2,1)S(1)}) fusion(s32[1024]{0:T(1024)S(1)} %get-tuple-element.20, s32[2048]{0:T(1024)S(1)} %get-tuple-element.18, s32[1024]{0:T(1024)S(1)} %get-tuple-element.19, s32[2048]{0:T(1024)S(1)} %get-tuple-element.17), kind=kLoop, calls=%fused_computation.16 | loop fusion | flops 39845888 | bytes 8413184 | tf_op jit(solution)/shard_map/convert.1
  175.4 1.4 fusion.14
  176.7 0.1 div.46
  176.8 0.1 reduce_sum.29
  177.0 0.1 mul.199
  177.1 0.1 broadcast_divide_fusion
  177.2 0.0 copy-start.2
  177.2 0.6 broadcast_multiply_fusion
  177.8 6.1 %broadcast_in_dim.17 = f32[2,64,16,4,3,128]{5,4,3,2,1,0:T(4,128)} broadcast(f32[2,64,16,3,128]{4,3,2,1,0:T(4,128)S(1)} %broadcast_multiply_fusion), dimensions={0,1,2,4,5} | broadcast | bytes 15728640 | tf_op jit(solution)/shard_map/broadcast_in_dim | solution.py:52
  183.9 0.0 copy-done.2
  183.9 57.7 %scatter_custom_fusion = f32[8192,384]{1,0:T(8,128)} fusion(s32[8192]{0:T(1024)S(1)} %reshape.217, f32[1024,8,3,128]{3,2,1,0:T(4,128)} %bitcast.115, f32[]{:T(128)} %constant.87.clone.1), kind=kCustom, calls=%fused_computation.2 | custom fusion | flops 3145728 | bytes 25165828 | tf_op jit(solution)/shard_map/scatter-add | solution.py:55
  241.5 12.6 %copy.54 = f32[8192,384]{0,1:T(8,128)} copy(f32[8192,384]{1,0:T(8,128)} %scatter_custom_fusion) | data formatting | bytes 25165824 | tf_op jit(solution)/shard_map/scatter-add | solution.py:55
  254.1 22.5 %copy.75 = f32[48,8,8,1024]{3,2,1,0:T(8,128)} copy(f32[48,8,8,1024]{3,1,2,0:T(8,128)} %bitcast.117) | data formatting | bytes 25165824
  276.6 0.0 copy-start.1
  276.6 7.7 %fusion.25 = f32[1024,3,128,1]{0,2,3,1:T(8,128)S(1)} fusion(f32[8,1024,3,128]{1,0,3,2:T(8,128)} %bitcast.116, bf16[8,128,128]{1,0,2:T(8,128)(2,1)S(1)} %copy.55), kind=kOutput, calls=%fused_computation.41 | convolution fusion | flops 4831838208 | bytes 14417920 | tf_op jit(solution)/shard_map/kvcq,kwq->vcw/dot_general | solution.py:87
  284.3 1.6 copy.56
  285.9 0.0 all-reduce.3.cloned.1.call-update
  286.0 260.9 %all-reduce.3.cloned.1.call-done = f32[1024,384]{1,0:T(8,128)} async-done(((f32[1024,384]{1,0:T(8,128)}), f32[1024,384]{1,0:T(8,128)}) %all-reduce.3.cloned.1.call-update) | async-done | bytes 1572880
  546.8 1.3 constant_dynamic-slice_fusion
  548.1 1.3 dynamic-slice.2
  549.5 0.0 copy-done.1
  (13 shorter events, 0.1 us)
Async XLA Ops:
  7.2 118.4 %copy-start = (bf16[64,2048]{1,0:T(8,128)(2,1)S(1)}, bf16[64,2048]{1,0:T(8,128)(2,1)}, u32[]{:S(2)}) copy-start(bf16[64,2048]{1,0:T(8,128)(2,1)} %param.9) | copy-start | bytes 786436
  7.2 539.7 %all-reduce.3.cloned.1.call-start = ((), (), s32[]{:S(2)}) async-start(), calls=%async_computation | async-start | bytes 3145728
  97.4 28.1 %copy-start.3 = (s32[2]{0:T(128)S(1)}, s32[2]{0:T(128)}, u32[]{:S(2)}) copy-start(s32[2]{0:T(128)} %param.10) | copy-start | bytes 28
  177.2 6.7 %copy-start.2 = (f32[2,64]{1,0:T(2,128)}, f32[2,64]{1,0:T(2,128)S(1)}, u32[]{:S(2)}) copy-start(f32[2,64]{1,0:T(2,128)S(1)} %broadcast_divide_fusion) | copy-start | bytes 1540
  276.6 272.8 %copy-start.1 = (bf16[64,2048]{1,0:T(8,128)(2,1)S(1)}, bf16[64,2048]{1,0:T(8,128)(2,1)}, u32[]{:S(2)}) copy-start(bf16[64,2048]{1,0:T(8,128)(2,1)} %param.9) | copy-start | bytes 786436
Sparse Core Ops, SparseCore 0:
  286.1 260.7 all-reduce.2
where the time goes:
time: 568 us; the launch traced here: 557 us
  waiting for transfers between devices  261 us (46%)
  other arithmetic  124 us (22%)
  local copies, waits for them, and re-layouts  113 us (20%)
  blocking collectives  30.7 us (5%)
  between operations  14.6 us (3%)
  matrix products  13.4 us (2%)
    unnamed x2, waiting for transfers between devices  261 us
    scatter-add x1, other arithmetic, score_group(): jax.ops.segment_sum(rows_all.reshape(-1, 3 * blk_width), row_ids.reshape(...  57.7 us
    another operation x2, other arithmetic  49.6 us
    gather x2, local copies, waits for them, and re-layouts, score_group(): picked = jnp.take(table_rows, row_ids.reshape(-1), axis=0)  40.5 us
    all_gather x1, blocking collectives, local(): slab_piece = lax.all_gather(ref_map, 'slab', axis=0, tiled=True)  30.7 us
    unnamed x14, local copies, waits for them, and re-layouts  29.3 us
    reduce_sum x1, other arithmetic, score_group(): projection = jnp.sum(picked.astype(jnp.float32), axis=3)  14.8 us
    scatter-add x1, local copies, waits for them, and re-layouts, score_group(): jax.ops.segment_sum(rows_all.reshape(-1, 3 * blk_width), row_ids.reshape(...  12.6 us
  transfers between devices with their start and end apart: 1, of which 1 were waited for; matrix products, arithmetic and copies ran while one was open for 0% of the time, Pallas kernels for 0%

commit v1 on v0

v1 whole, which is shorter than its diff:
```python
import jax
import jax.numpy as jnp
import numpy as np
from jax import lax
from jax.experimental import pallas as pl
from jax.experimental.pallas import tpu as pltpu
from jax.sharding import PartitionSpec as P

LINE = 256
PLINES = 8
SIDE = 32
BW = 128
TAPS = 4
KINDS = 8
CAND = 64
PB = 16
NBLK = 1024
MESH = pl.DeviceIdType.MESH
VMEM = pltpu.VMEM
F32 = jnp.float32
BF16 = jnp.bfloat16
NT = (((1,), (1,)), ((), ()))
TN = (((0,), (0,)), ((), ()))


def line_table():
    fx = np.arange(LINE) - LINE // 2
    sx = np.arange(SIDE) - SIDE // 2
    ang = 2.0 * np.pi / LINE * ((fx[:, None] * sx[None, :]) % LINE)
    cos, sin = np.cos(ang), np.sin(ang)
    one = np.zeros((2, 2, BW, 2, SIDE))
    one[:, 0, :, 0] = cos.reshape(2, BW, SIDE)
    one[:, 1, :, 0] = -sin.reshape(2, BW, SIDE)
    one[:, 0, :, 1] = sin.reshape(2, BW, SIDE)
    one[:, 1, :, 1] = cos.reshape(2, BW, SIDE)
    both = np.zeros((2, 2, 2, BW, 2, 2, SIDE))
    both[0, :, :, :, 0] = one
    both[1, :, :, :, 1] = one
    return both.reshape(8 * BW, 4 * SIDE)


def across_table():
    fy = np.arange(PLINES) - PLINES // 2
    sy = np.arange(SIDE) - SIDE // 2
    ang = 2.0 * np.pi / LINE * ((fy[None, :] * sy[:, None]) % LINE)
    full = np.zeros((SIDE, SIDE, PLINES, 2, SIDE))
    for s in range(SIDE):
        full[:, s, :, 0, s] = np.cos(ang)
        full[:, s, :, 1, s] = -np.sin(ang)
    return full.reshape(SIDE * SIDE, PLINES * 2 * SIDE)


def gather_kernel(piece, full, send_sem, recv_sem, own_sem):
    p = lax.axis_index("particle")
    s = lax.axis_index("slab")
    x_lo = lax.rem(p // 2, 2)
    x_hi = s // 4

    def peer(d):
        other = lax.rem(s + d, 8)
        apart = other // 4 - x_hi
        return (p + apart * apart * (2 - 4 * x_lo), other)

    barrier = pltpu.get_barrier_semaphore()
    for d in range(1, 8):
        pl.semaphore_signal(barrier, inc=1, device_id=peer(d), device_id_type=MESH)
    own = pltpu.make_async_copy(piece, full.at[s], own_sem)
    own.start()
    pl.semaphore_wait(barrier, 7)
    sends = []
    for d in (6, 2, 5, 3, 7, 1, 4):
        copy = pltpu.make_async_remote_copy(
            src_ref=piece,
            dst_ref=full.at[s],
            send_sem=send_sem.at[d],
            recv_sem=recv_sem.at[d],
            device_id=peer(d),
            device_id_type=MESH,
        )
        copy.start()
        sends.append(copy)
    own.wait()
    for d in range(1, 8):
        source = lax.rem(s + 8 - d, 8)
        pltpu.make_async_remote_copy(
            src_ref=piece,
            dst_ref=full.at[source],
            send_sem=send_sem.at[d],
            recv_sem=recv_sem.at[d],
            device_id=peer(d),
            device_id_type=MESH,
        ).wait_recv()
    for copy in sends:
        copy.wait_send()


def split(v):
    hi = v.astype(BF16)
    return hi, (v - hi.astype(F32)).astype(BF16)


def match_kernel(
    rid, cls, blk, kind, refs, bank, img, ctf, fx, fy,
    sums, post_out,
    table, inter, proj, cross, hist, rows, parts,
):
    inter[pl.ds(0, NBLK, stride=2), :] = refs[:, :BW].astype(F32)
    inter[pl.ds(1, NBLK, stride=2), :] = refs[:, BW:].astype(F32)
    for k in range(KINDS):
        weight = bank[k]

        @pl.loop(0, 4)
        def _(step):
            lhs = inter[pl.ds(pl.multiple_of(step * 512, 512), 512), :].astype(BF16)
            out = jnp.dot(lhs, weight, preferred_element_type=F32)
            start = pl.multiple_of(k * 2 * NBLK + step * 512, 512)
            table[pl.ds(start, 512), :] = out.astype(BF16).astype(F32)

    lanes = lax.broadcasted_iota(jnp.int32, (16, 64), 1)
    which = lax.broadcasted_iota(jnp.int32, (16, 64), 0)
    pick = jnp.where(which == 0, cls[0], cls[1])
    onehot = (lanes == pick).astype(F32).astype(BF16)
    gain = jnp.dot(onehot, ctf[...], preferred_element_type=F32)
    pixel = img[...].astype(F32)
    scaled = []
    for i in range(2):
        g = gain[i : i + 1]
        ca = g * pixel[i, 0:1]
        cb = g * pixel[i, 1:2]
        scaled.append((ca, cb))
        for c, row in enumerate((ca, cb, g * g)):
            for p in range(PB):
                parts[pl.ds(c * 32 + i * PB + p, 1), :] = row[:, p * BW : (p + 1) * BW]
    both = jnp.concatenate(split(parts[...]), axis=0)
    for k in range(KINDS):
        out = lax.dot_general(both, bank[k], NT, preferred_element_type=F32)
        out = out[:96] + out[96:]
        for c in range(3):
            rows[c, pl.ds(k, 32, stride=KINDS), :] = out[c * 32 : (c + 1) * 32]

    @pl.loop(0, 32)
    def _(ip):
        @pl.loop(0, 4)
        def _(part):
            for u in range(16):
                j = part * 16 + u
                taken = [table[pl.ds(pl.multiple_of(rid[ip, t * CAND + j] * 2, 2), 2), :] for t in range(TAPS)]
                total = (taken[0] + taken[1]) + (taken[2] + taken[3])
                proj[pl.ds(pl.multiple_of(ip * 128 + j * 2, 2), 2), :] = total

    for i in range(2):
        ca, cb = scaled[i]
        for p in range(PB):
            a = ca[:, p * BW : (p + 1) * BW]
            b = cb[:, p * BW : (p + 1) * BW]
            start = (i * PB + p) * 2 * CAND
            u = proj[pl.ds(start, CAND, stride=2), :]
            w = proj[pl.ds(start + 1, CAND, stride=2), :]
            at = pl.ds(i * CAND, CAND)
            cross[at, pl.ds(p * 256, 128)] = (a * u + b * w).astype(BF16)
            cross[at, pl.ds(p * 256 + 128, 128)] = (b * u - a * w).astype(BF16)

    along = [
        jnp.dot(cross[:, g * 1024 : (g + 1) * 1024], fx[...], preferred_element_type=F32)
        for g in range(4)
    ]
    along = jnp.concatenate(along, axis=1)
    hi, lo = split(along)
    scores = lax.dot_general(fy[...], hi, NT, preferred_element_type=F32)
    scores = scores + lax.dot_general(fy[...], lo, NT, preferred_element_type=F32)
    energy = jnp.sum(scores * scores, axis=0, keepdims=True) * (1.0 / (SIDE * SIDE))
    lane = lax.broadcasted_iota(jnp.int32, (1, 128), 1)
    first = lane < CAND
    sum0 = jnp.sum(jnp.where(first, energy, 0.0), axis=1, keepdims=True)
    sum1 = jnp.sum(jnp.where(first, 0.0, energy), axis=1, keepdims=True)
    post = CAND * energy / (jnp.where(first, sum0, sum1) + 1e-6)
    post_out[...] = post
    turned = jnp.concatenate([post[:, CAND:], post[:, :CAND]], axis=1)
    weights = (jnp.where(first, post, turned), jnp.where(first, turned, post))

    row_id = lax.broadcasted_iota(jnp.int32, (64, 256), 0)
    col_id = lax.broadcasted_iota(jnp.int32, (128, 256), 0)
    for i in range(2):
        w2 = jnp.concatenate([weights[i], weights[i]], axis=1)
        w_hi = w2.astype(BF16).astype(F32)
        w_lo = w2 - w_hi

        @pl.loop(0, PB)
        def _(p):
            ip = i * PB + p
            v = blk[pl.ds(ip, 1), :]
            k = kind[pl.ds(ip, 1), :]
            high = ((v >> 5) & 1) * 4 + ((v >> 4) & 1) * 2 + ((v >> 6) & 1)
            low = ((v >> 2) & 3) * 32 + (v >> 7) * 4 + (v & 3)
            hit = row_id == high * KINDS + k
            left = jnp.concatenate(
                [jnp.where(hit, w_hi, 0.0).astype(BF16), jnp.where(hit, w_lo, 0.0).astype(BF16)], axis=0
            )
            right = jnp.where(col_id == low, 1.0, 0.0).astype(BF16)
            out = lax.dot_general(left, right, NT, preferred_element_type=F32)
            out = out[:64] + out[64:]
            at = pl.ds(pl.multiple_of(ip * KINDS, KINDS), KINDS)
            for h in range(8):
                hist[at, pl.ds(h * 128, 128)] = out[h * 8 : (h + 1) * 8]

    d_hi, d_lo = split(jnp.concatenate([rows[c] for c in range(3)], axis=1))
    d_both = jnp.concatenate([d_hi, d_lo], axis=1)
    for h in range(8):
        at = pl.ds(h * 128, 128)
        h_hi, h_lo = split(hist[:, at].T)
        out = jnp.dot(h_hi, d_both, preferred_element_type=F32)
        sums[at, :] = out[:, :384] + out[:, 384:] + jnp.dot(h_lo, d_hi, preferred_element_type=F32)


def scatter_kernel(
    sums, data, weight,
    near, s1, a1, b1, s2a, s2b, a2, b2, s3, r3,
    near_s, near_r, xs, xr, ys, yr, x2s, x2r, y2s, y2r, zs, zr,
):
    p = lax.axis_index("particle")
    s = lax.axis_index("slab")
    z, x_lo, core = p // 4, lax.rem(p // 2, 2), lax.rem(p, 2)
    x_hi, y = s // 4, lax.rem(s, 4)
    x = x_hi * 2 + x_lo

    sibling = (p + 1 - 2 * core, s)

    def x_peer(d):
        to = lax.rem(x + d, 4)
        return to, (p + (lax.rem(to, 2) - x_lo) * 2, s + (to // 2 - x_hi) * 4)

    def y_peer(d):
        to = lax.rem(y + d, 4)
        return to, (p, s + to - y)

    def z_peer(d):
        to = lax.rem(z + d, 8)
        return to, (p + (to - z) * 4, s)

    peers = [sibling] + [x_peer(d)[1] for d in (1, 2, 3)] + [y_peer(d)[1] for d in (1, 2, 3)]
    peers += [z_peer(d)[1] for d in range(1, 8)]
    barrier = pltpu.get_barrier_semaphore()
    for peer in peers:
        pl.semaphore_signal(barrier, inc=1, device_id=peer, device_id_type=MESH)
    pl.semaphore_wait(barrier, len(peers))

    def send(src, dst, ssem, rsem, peer):
        copy = pltpu.make_async_remote_copy(
            src_ref=src, dst_ref=dst, send_sem=ssem, recv_sem=rsem, device_id=peer, device_id_type=MESH
        )
        copy.start()
        return copy

    order = [lax.rem(x + d, 4) for d in (2, 1, 3, 0)]
    done = []
    first = []
    for n, to in enumerate(order):
        first.append(send(sums.at[1 - core, to], near.at[to], near_s.at[n], near_r.at[n], sibling))
    last = []
    for n, d in enumerate((2, 1, 3, 0)):
        to = order[n]
        first[n].wait_recv()
        s1[to] = sums[core, to] + near[to]
        if d:
            last.append(send(s1.at[to, :, pl.ds(0, 16)], a1.at[d], xs.at[d], xr.at[d], x_peer(d)[1]))
    for d in (2, 1, 3):
        to, peer = y_peer(d)
        done.append(send(s1.at[:, to, pl.ds(16, 16)], b1.at[d], ys.at[d], yr.at[d], peer))
    for copy in last:
        copy.wait_recv()
    s2a[...] = (s1[x, :, 0:16, :] + a1[1]) + (a1[2] + a1[3])
    second = []
    for d in (2, 1, 3):
        to, peer = y_peer(d)
        second.append(send(s2a.at[to], a2.at[d], y2s.at[d], y2r.at[d], peer))
    for copy in done:
        copy.wait_recv()
    s2b[...] = (s1[:, y, 16:32, :] + b1[1]) + (b1[2] + b1[3])
    for d in (2, 1, 3):
        to, peer = x_peer(d)
        second.append(send(s2b.at[to], b2.at[d], x2s.at[d], x2r.at[d], peer))
    for copy in second[:3]:
        copy.wait_recv()
    low = (s2a[y] + a2[1]) + (a2[2] + a2[3])
    for n in range(4):
        s3[n] = low[n * 4 : (n + 1) * 4]
    for copy in second[3:]:
        copy.wait_recv()
    high = (s2b[x] + b2[1]) + (b2[2] + b2[3])
    for n in range(4):
        s3[4 + n] = high[n * 4 : (n + 1) * 4]
    third = []
    for d in (4, 3, 5, 2, 6, 1, 7):
        to, peer = z_peer(d)
        third.append(send(s3.at[to], r3.at[d], zs.at[d], zr.at[d], peer))
    for copy in third:
        copy.wait_recv()
    total = s3[z]
    for d in range(1, 8):
        total = total + r3[d]
    data[...] = total[:, :256]
    weight[...] = total[:, 256:]
    for copy in first + last + done + second + third:
        copy.wait_send()


def whole():
    return pl.BlockSpec(memory_space=VMEM)


def local(ref_map, images, ctf_table, ctf_class, block_index, interp_kind, interp_bank):
    full = pl.pallas_call(
        gather_kernel,
        out_shape=jax.ShapeDtypeStruct((8, NBLK // 8, 2 * BW), BF16),
        in_specs=[whole()],
        out_specs=whole(),
        scratch_shapes=[
            pltpu.SemaphoreType.DMA((8,)),
            pltpu.SemaphoreType.DMA((8,)),
            pltpu.SemaphoreType.DMA,
        ],
        compiler_params=pltpu.CompilerParams(collective_id=0, has_side_effects=True),
        name="gather_map",
    )(ref_map)
    blk = jnp.transpose(block_index, (0, 2, 3, 1)).reshape(32, TAPS * CAND)
    kind = jnp.transpose(interp_kind, (0, 2, 3, 1)).reshape(32, TAPS * CAND)
    rid = kind * NBLK + blk
    smem = pl.BlockSpec(memory_space=pltpu.SMEM)
    sums, post = pl.pallas_call(
        match_kernel,
        out_shape=[
            jax.ShapeDtypeStruct((NBLK, 384), F32),
            jax.ShapeDtypeStruct((1, 128), F32),
        ],
        in_specs=[smem, smem] + [whole()] * 8,
        out_specs=[whole()] * 2,
        scratch_shapes=[
            VMEM((2 * KINDS * NBLK, BW), F32),
            VMEM((2 * NBLK, BW), F32),
            VMEM((4096, BW), F32),
            VMEM((128, 4096), BF16),
            VMEM((256, NBLK), F32),
            VMEM((3, 256, BW), F32),
            VMEM((96, BW), F32),
        ],
        compiler_params=pltpu.CompilerParams(vmem_limit_bytes=48 * 1024 * 1024),
        name="match",
    )(
        rid, ctf_class, blk, kind, full.reshape(NBLK, 2 * BW), interp_bank, images, ctf_table,
        jnp.asarray(line_table(), BF16), jnp.asarray(across_table(), BF16),
    )
    dma = pltpu.SemaphoreType.DMA
    data_map, weight_map = pl.pallas_call(
        scatter_kernel,
        out_shape=[
            jax.ShapeDtypeStruct((4, 256), F32),
            jax.ShapeDtypeStruct((4, 128), F32),
        ],
        in_specs=[whole()],
        out_specs=[whole()] * 2,
        scratch_shapes=[
            VMEM((4, 4, 32, 384), F32),
            VMEM((4, 4, 32, 384), F32),
            VMEM((4, 4, 16, 384), F32),
            VMEM((4, 4, 16, 384), F32),
            VMEM((4, 16, 384), F32),
            VMEM((4, 16, 384), F32),
            VMEM((4, 16, 384), F32),
            VMEM((4, 16, 384), F32),
            VMEM((8, 4, 384), F32),
            VMEM((8, 4, 384), F32),
            dma((4,)), dma((4,)), dma((4,)), dma((4,)), dma((4,)), dma((4,)),
            dma((4,)), dma((4,)), dma((4,)), dma((4,)), dma((8,)), dma((8,)),
        ],
        compiler_params=pltpu.CompilerParams(
            collective_id=1, has_side_effects=True, vmem_limit_bytes=32 * 1024 * 1024
        ),
        name="scatter_sums",
    )(sums.reshape(2, 4, 4, 32, 384))
    return (data_map, weight_map, post.reshape(2, CAND))


def solution(mesh):
    in_specs = (
        P("slab", None),
        P(("particle", "slab"), None, None),
        P(),
        P(("particle", "slab")),
        P(("particle", "slab"), None, None, None),
        P(("particle", "slab"), None, None, None),
        P(),
    )
    out_specs = (
        P(("particle", "slab"), None),
        P(("particle", "slab"), None),
        P(("particle", "slab"), None),
    )
    return jax.shard_map(local, mesh=mesh, in_specs=in_specs, out_specs=out_specs, check_vma=False)
```

time: 568 us -> 88.2 us (0.16)
  the two profiles are of different devices: /device:TPU:2 before, /device:TPU:1 now
where the time goes in v1:
time: 88.2 us; the launch traced here: 87.7 us
  Pallas kernels  75.7 us (86%)
  local copies, waits for them, and re-layouts  10.7 us (12%)
    pallas_call x1, Pallas kernels, local(): pl.pallas_call(match_kernel, out_shape=[jax.ShapeDtypeStruct((NBLK, 384),...  37.9 us
    pallas_call x1, Pallas kernels, local(): pl.pallas_call(scatter_kernel, out_shape=[jax.ShapeDtypeStruct((4, 256),...  22.6 us
    pallas_call x1, Pallas kernels, local(): pl.pallas_call(gather_kernel, out_shape=jax.ShapeDtypeStruct((8, NBLK //...  15.2 us
    unnamed x16, local copies, waits for them, and re-layouts  7.65 us

profile of v1, /device:TPU:1, one launch (start us, length us, event | category | flops | bytes accessed | tf_op | source)
XLA Modules:
  0.0 87.7 jit_solution(5122377289559261615)
XLA Ops:
  0.6 0.9 %reshape.21.kind = s32[32,256]{1,0:T(8,128)S(1)} reshape(s32[2,16,4,64]{3,2,1,0:T(4,128)} %bitcast.6) | data formatting | bytes 65536 | tf_op jit(solution)/shard_map/reshape | solution.py:326
  1.6 0.9 %reshape.22.blk = s32[32,256]{1,0:T(8,128)S(1)} reshape(s32[2,16,4,64]{3,2,1,0:T(4,128)} %bitcast.7) | data formatting | bytes 65536 | tf_op jit(solution)/shard_map/reshape | solution.py:325
  2.5 15.2 %gather_map.1 = bf16[8,128,256]{2,1,0:T(8,128)(2,1)} custom-call(bf16[128,256]{1,0:T(8,128)(2,1)} %piece.1), custom_call_target="tpu_custom_call" | custom-call | tf_op jit(solution)/shard_map/gather_map/pallas_call | solution.py:312
  17.7 0.0 copy-start
  17.7 1.0 %copy-done = bf16[8,128,256]{2,1,0:T(8,128)(2,1)S(1)} copy-done((bf16[8,128,256]{2,1,0:T(8,128)(2,1)S(1)}, bf16[8,128,256]{2,1,0:T(8,128)(2,1)}, u32[]{:S(2)}) %copy-start) | copy-done | bytes 524312
  18.8 0.0 copy-start.1
  18.8 1.2 %copy-done.1 = bf16[1024,512]{1,0:T(8,128)(2,1)S(1)} copy-done((bf16[1024,512]{1,0:T(8,128)(2,1)S(1)}, bf16[1024,512]{1,0:T(8,128)(2,1)}, u32[]{:S(2)}) %copy-start.1) | copy-done | bytes 1048600
  20.0 0.0 copy-start.2
  20.0 0.9 %copy-done.2 = bf16[8,128,128]{2,1,0:T(8,128)(2,1)S(1)} copy-done((bf16[8,128,128]{2,1,0:T(8,128)(2,1)S(1)}, bf16[8,128,128]{2,1,0:T(8,128)(2,1)}, u32[]{:S(2)}) %copy-start.2) | copy-done | bytes 262168
  20.9 0.0 copy-start.3
  20.9 0.9 %copy-done.3 = bf16[64,2048]{1,0:T(8,128)(2,1)S(1)} copy-done((bf16[64,2048]{1,0:T(8,128)(2,1)S(1)}, bf16[64,2048]{1,0:T(8,128)(2,1)}, u32[]{:S(2)}) %copy-start.3) | copy-done | bytes 262168
  21.9 0.0 copy-start.4
  21.9 0.9 %copy-done.4 = bf16[1024,128]{1,0:T(8,128)(2,1)S(1)} copy-done((bf16[1024,128]{1,0:T(8,128)(2,1)S(1)}, bf16[1024,128]{1,0:T(8,128)(2,1)}, u32[]{:S(2)}) %copy-start.4) | copy-done | bytes 262168
  22.8 0.0 copy-start.5
  22.8 0.7 copy-done.5
  23.5 0.0 copy-start.6
  23.5 0.7 copy-done.6
  24.2 37.9 %match.1 = (f32[1024,384]{1,0:T(8,128)S(1)}, f32[1,128]{1,0:T(1,128)S(1)}) custom-call(s32[32,256]{1,0:T(8,128)S(1)} %multiply_add_fusion.rid, s32[2]{0:T(128)S(1)} %copy-done.6, s32[32,256]{1,0:T(8,128)S(1)} %reshape.22.blk, s32[32,256]{1,0:T(8,128)S(1)} %reshape.21.kind, bf16[1024,256]{1,0:T(8,128)(2,1)S(1)} %bitcast.4, ...), custom_call_target="tpu_custom_call" | custom-call | tf_op jit(solution)/shard_map/match/pallas_call | solution.py:329
  62.1 22.6 %scatter_sums.1 = (f32[4,256]{1,0:T(4,128)S(1)}, f32[4,128]{1,0:T(4,128)S(1)}) custom-call(f32[2,4,4,32,384]{4,3,2,1,0:T(8,128)S(1)} %bitcast.5), custom_call_target="tpu_custom_call" | custom-call | tf_op jit(solution)/shard_map/scatter_sums/pallas_call | solution.py:353
  84.7 0.5 broadcast.3
  85.2 0.7 reduce.3
  85.9 0.6 reshape.25
  86.5 0.6 copy.14
  87.1 0.6 copy.15
  (1 shorter events, 0.0 us)
Async XLA Ops:
  17.7 1.0 %copy-start = (bf16[8,128,256]{2,1,0:T(8,128)(2,1)S(1)}, bf16[8,128,256]{2,1,0:T(8,128)(2,1)}, u32[]{:S(2)}) copy-start(bf16[8,128,256]{2,1,0:T(8,128)(2,1)} %gather_map.1) | copy-start | bytes 1572868
  18.8 1.2 %copy-start.1 = (bf16[1024,512]{1,0:T(8,128)(2,1)S(1)}, bf16[1024,512]{1,0:T(8,128)(2,1)}, u32[]{:S(2)}) copy-start(bf16[1024,512]{1,0:T(8,128)(2,1)} %constant.7.clone.fy) | copy-start | bytes 3145732
  20.0 0.9 %copy-start.2 = (bf16[8,128,128]{2,1,0:T(8,128)(2,1)S(1)}, bf16[8,128,128]{2,1,0:T(8,128)(2,1)}, u32[]{:S(2)}) copy-start(bf16[8,128,128]{2,1,0:T(8,128)(2,1)} %bank.1) | copy-start | bytes 786436
  20.9 0.9 %copy-start.3 = (bf16[64,2048]{1,0:T(8,128)(2,1)S(1)}, bf16[64,2048]{1,0:T(8,128)(2,1)}, u32[]{:S(2)}) copy-start(bf16[64,2048]{1,0:T(8,128)(2,1)} %ctf.1) | copy-start | bytes 786436
  21.9 0.9 %copy-start.4 = (bf16[1024,128]{1,0:T(8,128)(2,1)S(1)}, bf16[1024,128]{1,0:T(8,128)(2,1)}, u32[]{:S(2)}) copy-start(bf16[1024,128]{1,0:T(8,128)(2,1)} %constant.6.clone.fx) | copy-start | bytes 786436
  22.8 0.7 copy-start.5
  23.5 0.7 copy-start.6

commit v2 on v0

v2 whole, which is shorter than its diff:
```python
import jax
import jax.numpy as jnp
import numpy as np
from jax import lax
from jax.experimental import pallas as pl
from jax.experimental.pallas import tpu as pltpu
from jax.sharding import PartitionSpec as P

LINE = 256
PLINES = 8
SIDE = 32
BW = 128
TAPS = 4
KINDS = 8
CAND = 64
PB = 16
NBLK = 1024
MESH = pl.DeviceIdType.MESH
VMEM = pltpu.VMEM
F32 = jnp.float32
BF16 = jnp.bfloat16
NT = (((1,), (1,)), ((), ()))


def line_table():
    fx = np.arange(LINE) - LINE // 2
    sx = np.arange(SIDE) - SIDE // 2
    ang = 2.0 * np.pi / LINE * ((fx[:, None] * sx[None, :]) % LINE)
    cos, sin = np.cos(ang), np.sin(ang)
    one = np.zeros((2, 2, BW, 2, SIDE))
    one[:, 0, :, 0] = cos.reshape(2, BW, SIDE)
    one[:, 1, :, 0] = -sin.reshape(2, BW, SIDE)
    one[:, 0, :, 1] = sin.reshape(2, BW, SIDE)
    one[:, 1, :, 1] = cos.reshape(2, BW, SIDE)
    both = np.zeros((2, 2, 2, BW, 2, 2, SIDE))
    both[0, :, :, :, 0] = one
    both[1, :, :, :, 1] = one
    return both.reshape(8 * BW, 4 * SIDE)


def across_table():
    fy = np.arange(PLINES) - PLINES // 2
    sy = np.arange(SIDE) - SIDE // 2
    ang = 2.0 * np.pi / LINE * ((fy[None, :] * sy[:, None]) % LINE)
    full = np.zeros((SIDE, SIDE, PLINES, 2, SIDE))
    for s in range(SIDE):
        full[:, s, :, 0, s] = np.cos(ang)
        full[:, s, :, 1, s] = -np.sin(ang)
    return full.reshape(SIDE * SIDE, PLINES * 2 * SIDE)


def split(v):
    hi = v.astype(BF16)
    return hi, (v - hi.astype(F32)).astype(BF16)


def refine_kernel(
    piece, img_h, ctf_h, cls_h, blk_h, kind_h, bank_h, fx_h, fy_h,
    data, weight, post_out,
    img, ctf, cls, blk, kind, bank, fx, fy, own_sem,
    full, table, parts, rows, rid_v, rid, left, right,
    proj, cross, hist, gather_s, gather_r,
    sums, near, s1, a1, b1, s2a, s2b, a2, b2, s3, r3,
    near_s, near_r, xs, xr, ys, yr, x2s, x2r, y2s, y2r, zs, zr,
):
    p = lax.axis_index("particle")
    s = lax.axis_index("slab")
    z, x_lo, core = p // 4, lax.rem(p // 2, 2), lax.rem(p, 2)
    x_hi, y = s // 4, lax.rem(s, 4)
    x = x_hi * 2 + x_lo

    sibling = (p + 1 - 2 * core, s)

    def x_peer(d):
        to = lax.rem(x + d, 4)
        return to, (p + (lax.rem(to, 2) - x_lo) * 2, s + (to // 2 - x_hi) * 4)

    def y_peer(d):
        to = lax.rem(y + d, 4)
        return to, (p, s + to - y)

    def z_peer(d):
        to = lax.rem(z + d, 8)
        return to, (p + (to - z) * 4, s)

    def map_peer(d):
        other = lax.rem(s + d, 8)
        apart = other // 4 - x_hi
        return (p + apart * apart * (2 - 4 * x_lo), other)

    def send(src, dst, ssem, rsem, peer):
        copy = pltpu.make_async_remote_copy(
            src_ref=src, dst_ref=dst, send_sem=ssem, recv_sem=rsem, device_id=peer, device_id_type=MESH
        )
        copy.start()
        return copy

    peers = [sibling] + [x_peer(d)[1] for d in (1, 2, 3)] + [z_peer(d)[1] for d in range(1, 8)]
    peers += [map_peer(d) for d in range(1, 8)]
    barrier = pltpu.get_barrier_semaphore()
    for peer in peers:
        pl.semaphore_signal(barrier, inc=1, device_id=peer, device_id_type=MESH)
    pairs = [
        (blk_h, blk), (kind_h, kind), (img_h, img), (ctf_h, ctf), (cls_h, cls), (bank_h, bank),
        (piece, full.at[s]), (fx_h, fx), (fy_h, fy),
    ]
    loads = [pltpu.make_async_copy(a, b, own_sem.at[n]) for n, (a, b) in enumerate(pairs)]
    for load in loads:
        load.start()
    pl.semaphore_wait(barrier, len(peers))
    sends = []
    for d in (6, 2, 5, 3, 7, 1, 4):
        sends.append(send(piece, full.at[s], gather_s.at[d], gather_r.at[d], map_peer(d)))

    loads[0].wait()
    loads[1].wait()
    number = kind[...] * NBLK + blk[...]
    for h in range(2):
        pair = jnp.concatenate([number[:, 2 * h, :], number[:, 2 * h + 1, :]], axis=1)
        rid_v[pl.ds(h * 32, 32), :] = pair
    to_scalar = pltpu.make_async_copy(rid_v, rid, own_sem.at[len(pairs)])
    to_scalar.start()

    for load in loads[2:6]:
        load.wait()
    lanes = lax.broadcasted_iota(jnp.int32, (16, 64), 1)
    which = lax.broadcasted_iota(jnp.int32, (16, 64), 0)
    pick = jnp.where(which == 0, cls[0], cls[1])
    onehot = (lanes == pick).astype(F32).astype(BF16)
    gain = jnp.dot(onehot, ctf[...], preferred_element_type=F32)
    pixel = img[...].astype(F32)
    for i in range(2):
        g = gain[i : i + 1]
        for c, row in enumerate((g * pixel[i, 0:1], g * pixel[i, 1:2], g * g)):
            for b in range(PB):
                parts[pl.ds(c * 32 + i * PB + b, 1), :] = row[:, b * BW : (b + 1) * BW]
    both = jnp.concatenate(split(parts[...]), axis=0)
    for k in range(KINDS):
        out = lax.dot_general(both, bank[k], NT, preferred_element_type=F32)
        out = out[:96] + out[96:]
        for c in range(3):
            rows[c, pl.ds(k, 32, stride=KINDS), :] = out[c * 32 : (c + 1) * 32]

    row_id = lax.broadcasted_iota(jnp.int32, (64, 128), 0)
    col_id = lax.broadcasted_iota(jnp.int32, (128, 128), 0)

    @pl.loop(0, 32)
    def _(ip):
        for h in range(2):
            v = rid_v[pl.ds(h * 32 + ip, 1), :]
            high = ((v >> 5) & 1) * 4 + ((v >> 4) & 1) * 2 + ((v >> 6) & 1)
            low = ((v >> 2) & 3) * 32 + ((v >> 7) & 7) * 4 + (v & 3)
            at = pl.ds(h * 128, 128)
            left[ip, :, at] = jnp.where(row_id == high * KINDS + (v >> 10), 1.0, 0.0).astype(BF16)
            right[ip, :, at] = jnp.where(col_id == low, 1.0, 0.0).astype(BF16)

    def map_piece(source):
        lhs = jnp.concatenate([full[source, :, :BW], full[source, :, BW:]], axis=0)
        for k in range(0, KINDS, 2):
            out = jnp.dot(lhs, jnp.concatenate([bank[k], bank[k + 1]], axis=1), preferred_element_type=F32)
            for h in range(2):
                at = pl.ds(pl.multiple_of((k + h) * NBLK + source * BW, BW), BW)
                for c in range(2):
                    half = out[c * BW : (c + 1) * BW, h * BW : (h + 1) * BW]
                    table[c, at, :] = half.astype(BF16).astype(F32)

    loads[6].wait()
    map_piece(s)

    @pl.loop(1, 8)
    def _(d):
        source = lax.rem(s + 8 - d, 8)
        pltpu.make_async_remote_copy(
            src_ref=piece, dst_ref=full.at[source], send_sem=gather_s.at[d], recv_sem=gather_r.at[d],
            device_id=map_peer(d), device_id_type=MESH,
        ).wait_recv()
        map_piece(source)

    to_scalar.wait()
    loads[7].wait()
    loads[8].wait()

    def gather(i, b):
        ip = i * PB + b
        for j in range(CAND):
            taps = [rid[h * 32 + ip, q * CAND + j] for h in range(2) for q in range(2)]
            for c in range(2):
                taken = [table[c, r] for r in taps]
                total = (taken[0] + taken[1]) + (taken[2] + taken[3])
                proj[c, pl.ds(pl.multiple_of(b * CAND, CAND) + j, 1), :] = total.reshape(1, BW)

    def posterior(i):
        for b in range(PB):
            ca = parts[pl.ds(i * PB + b, 1), :]
            cb = parts[pl.ds(32 + i * PB + b, 1), :]
            u = proj[0, pl.ds(b * CAND, CAND), :]
            w = proj[1, pl.ds(b * CAND, CAND), :]
            cross[:, pl.ds(b * 256, 128)] = (ca * u + cb * w).astype(BF16)
            cross[:, pl.ds(b * 256 + 128, 128)] = (cb * u - ca * w).astype(BF16)
        along = [
            jnp.dot(cross[:, g * 1024 : (g + 1) * 1024], fx[...], preferred_element_type=F32)
            for g in range(4)
        ]
        along = jnp.concatenate(along, axis=1)
        both = jnp.concatenate(split(along), axis=0)
        scores = lax.dot_general(fy[...], both, NT, preferred_element_type=F32)
        scores = scores[:, :CAND] + scores[:, CAND:]
        energy = jnp.sum(scores * scores, axis=0, keepdims=True) * (1.0 / (SIDE * SIDE))
        post = CAND * energy / (jnp.sum(energy, axis=1, keepdims=True) + 1e-6)
        post_out[pl.ds(i, 1), :] = post
        pair = jnp.concatenate([post, post, post, post], axis=1)
        return split(pair)

    def histogram(i, b, w_hi, w_lo):
        ip = i * PB + b
        hit = left[ip]
        hits = jnp.concatenate([hit * w_hi, hit * w_lo], axis=0)
        out = lax.dot_general(hits, right[ip], NT, preferred_element_type=F32)
        out = out[:64] + out[64:]
        at = pl.ds(pl.multiple_of(ip * KINDS, KINDS), KINDS)
        for h in range(8):
            hist[at, pl.ds(h * 128, 128)] = out[h * 8 : (h + 1) * 8]

    @pl.loop(0, PB)
    def _(b):
        gather(0, b)

    first = posterior(0)

    @pl.loop(0, PB)
    def _(b):
        gather(1, b)
        histogram(0, b, *first)

    second = posterior(1)

    @pl.loop(0, PB)
    def _(b):
        histogram(1, b, *second)

    d_hi, d_lo = split(jnp.concatenate([rows[c] for c in range(3)], axis=1))
    d_both = jnp.concatenate([d_hi, d_lo], axis=1)

    def map_sums(of_core, to):
        start = pl.multiple_of((of_core * 4 + to) * 128, 128)
        h_hi, h_lo = split(hist[:, pl.ds(start, 128)].T)
        out = jnp.dot(h_hi, d_both, preferred_element_type=F32)
        out = out[:, :384] + out[:, 384:] + jnp.dot(h_lo, d_hi, preferred_element_type=F32)
        return out.reshape(4, 32, 384)

    order = (2, 1, 3, 0)
    to_near = []
    for n, d in enumerate(order):
        to = lax.rem(x + d, 4)
        sums[to] = map_sums(1 - core, to)
        to_near.append(send(sums.at[to], near.at[to], near_s.at[n], near_r.at[n], sibling))
    last = []
    for n, d in enumerate(order):
        to, peer = x_peer(d)
        mine = map_sums(core, to)
        to_near[n].wait_recv()
        s1[to] = mine + near[to]
        if d:
            last.append(send(s1.at[to, :, pl.ds(0, 16)], a1.at[d], xs.at[d], xr.at[d], peer))
    done = []
    for d in (2, 1, 3):
        to, peer = y_peer(d)
        done.append(send(s1.at[:, to, pl.ds(16, 16)], b1.at[d], ys.at[d], yr.at[d], peer))
    for copy in last:
        copy.wait_recv()
    s2a[...] = (s1[x, :, 0:16, :] + a1[1]) + (a1[2] + a1[3])
    then = []
    for d in (2, 1, 3):
        to, peer = y_peer(d)
        then.append(send(s2a.at[to], a2.at[d], y2s.at[d], y2r.at[d], peer))
    for copy in done:
        copy.wait_recv()
    s2b[...] = (s1[:, y, 16:32, :] + b1[1]) + (b1[2] + b1[3])
    for d in (2, 1, 3):
        to, peer = x_peer(d)
        then.append(send(s2b.at[to], b2.at[d], x2s.at[d], x2r.at[d], peer))
    for copy in then[:3]:
        copy.wait_recv()
    low = (s2a[y] + a2[1]) + (a2[2] + a2[3])
    for n in range(4):
        s3[n] = low[n * 4 : (n + 1) * 4]
    for copy in then[3:]:
        copy.wait_recv()
    high = (s2b[x] + b2[1]) + (b2[2] + b2[3])
    for n in range(4):
        s3[4 + n] = high[n * 4 : (n + 1) * 4]
    third = []
    for d in (4, 3, 5, 2, 6, 1, 7):
        to, peer = z_peer(d)
        third.append(send(s3.at[to], r3.at[d], zs.at[d], zr.at[d], peer))
    for copy in third:
        copy.wait_recv()
    total = s3[z]
    for d in range(1, 8):
        total = total + r3[d]
    data[...] = total[:, :256]
    weight[...] = total[:, 256:]
    for copy in sends + to_near + last + done + then + third:
        copy.wait_send()


def local(ref_map, images, ctf_table, ctf_class, block_index, interp_kind, interp_bank):
    blk = jnp.transpose(block_index, (0, 2, 3, 1)).reshape(32, TAPS, CAND)
    kind = jnp.transpose(interp_kind, (0, 2, 3, 1)).reshape(32, TAPS, CAND)
    dma = pltpu.SemaphoreType.DMA
    i32 = jnp.int32
    return pl.pallas_call(
        refine_kernel,
        out_shape=[
            jax.ShapeDtypeStruct((4, 256), F32),
            jax.ShapeDtypeStruct((4, 128), F32),
            jax.ShapeDtypeStruct((2, CAND), F32),
        ],
        in_specs=[pl.BlockSpec(memory_space=pltpu.HBM)] * 9,
        out_specs=[pl.BlockSpec(memory_space=VMEM)] * 3,
        scratch_shapes=[
            VMEM((2, 2, 2048), BF16),
            VMEM((64, 2048), BF16),
            pltpu.SMEM((2,), i32),
            VMEM((32, TAPS, CAND), i32),
            VMEM((32, TAPS, CAND), i32),
            VMEM((KINDS, BW, BW), BF16),
            VMEM((1024, 128), BF16),
            VMEM((1024, 512), BF16),
            dma((10,)),
            VMEM((8, BW, 2 * BW), BF16),
            VMEM((2, KINDS * NBLK, BW), F32),
            VMEM((96, BW), F32),
            VMEM((3, 256, BW), F32),
            VMEM((64, 128), i32),
            pltpu.SMEM((64, 128), i32),
            VMEM((32, 64, 256), BF16),
            VMEM((32, 128, 256), BF16),
            VMEM((2, CAND * PB, BW), F32),
            VMEM((CAND, 4096), BF16),
            VMEM((256, NBLK), F32),
            dma((8,)), dma((8,)),
            VMEM((4, 4, 32, 384), F32),
            VMEM((4, 4, 32, 384), F32),
            VMEM((4, 4, 32, 384), F32),
            VMEM((4, 4, 16, 384), F32),
            VMEM((4, 4, 16, 384), F32),
            VMEM((4, 16, 384), F32),
            VMEM((4, 16, 384), F32),
            VMEM((4, 16, 384), F32),
            VMEM((4, 16, 384), F32),
            VMEM((8, 4, 384), F32),
            VMEM((8, 4, 384), F32),
            dma((4,)), dma((4,)), dma((4,)), dma((4,)), dma((4,)), dma((4,)),
            dma((4,)), dma((4,)), dma((4,)), dma((4,)), dma((8,)), dma((8,)),
        ],
        compiler_params=pltpu.CompilerParams(
            collective_id=0, has_side_effects=True, vmem_limit_bytes=56 * 1024 * 1024
        ),
        name="refine",
    )(
        ref_map, images, ctf_table, ctf_class, blk, kind, interp_bank,
        jnp.asarray(line_table(), BF16), jnp.asarray(across_table(), BF16),
    )


def solution(mesh):
    in_specs = (
        P("slab", None),
        P(("particle", "slab"), None, None),
        P(),
        P(("particle", "slab")),
        P(("particle", "slab"), None, None, None),
        P(("particle", "slab"), None, None, None),
        P(),
    )
    out_specs = (
        P(("particle", "slab"), None),
        P(("particle", "slab"), None),
        P(("particle", "slab"), None),
    )
    return jax.shard_map(local, mesh=mesh, in_specs=in_specs, out_specs=out_specs, check_vma=False)
```

time: 568 us -> 56.5 us (0.10)
  the two profiles are of different devices: /device:TPU:2 before, /device:TPU:1 now
where the time goes in v2:
time: 56.5 us; the launch traced here: 55.8 us
  Pallas kernels  52.6 us (93%)
  local copies, waits for them, and re-layouts  2.56 us (5%)
  between operations  0.65 us (1%)
    pallas_call x1, Pallas kernels, local(): pl.pallas_call(refine_kernel, out_shape=[jax.ShapeDtypeStruct((4, 256), F...  52.6 us
    unnamed x9, local copies, waits for them, and re-layouts  2.56 us

profile of v2, /device:TPU:1, one launch (start us, length us, event | category | flops | bytes accessed | tf_op | source)
XLA Modules:
  0.0 55.8 jit_solution(8841400089093896320)
XLA Ops:
  0.6 52.6 %refine.1 = (f32[4,256]{1,0:T(4,128)}, f32[4,128]{1,0:T(4,128)}, f32[2,64]{1,0:T(2,128)}) custom-call(bf16[128,256]{1,0:T(8,128)(2,1)} %piece.1, bf16[2,2,2048]{2,1,0:T(2,128)(2,1)} %img_h.1, bf16[64,2048]{1,0:T(8,128)(2,1)} %ctf_h.1, s32[2]{0:T(128)} %cls_h.1, s32[32,4,64]{2,1,0:T(4,128)} %bitcast.6, s32[32,4,64]{2,1,0:T(4,128)} %bitcast.7, ...), custom_call_target="tpu_custom_call" | custom-call | tf_op jit(solution)/shard_map/refine/pallas_call | solution.py:312
  53.2 0.0 copy-start
  53.2 0.7 %copy-done = f32[4,256]{1,0:T(4,128)S(1)} copy-done((f32[4,256]{1,0:T(4,128)S(1)}, f32[4,256]{1,0:T(4,128)}, u32[]{:S(2)}) %copy-start) | copy-done | bytes 4120
  53.9 0.0 copy-start.1
  53.9 0.6 %copy.15 = f32[4,256]{1,0:T(4,128)} copy(f32[4,256]{1,0:T(4,128)S(1)} %copy-done) | data formatting | bytes 8192
  54.5 0.1 copy-done.1
  54.6 0.0 copy-start.2
  54.6 0.6 %copy.16 = f32[4,128]{1,0:T(4,128)} copy(f32[4,128]{1,0:T(4,128)S(1)} %copy-done.1) | data formatting | bytes 4096
  55.1 0.1 copy-done.2
  55.2 0.6 %copy.17 = f32[2,64]{1,0:T(2,128)} copy(f32[2,64]{1,0:T(2,128)S(1)} %copy-done.2) | data formatting | bytes 1024
Async XLA Ops:
  53.2 0.7 %copy-start = (f32[4,256]{1,0:T(4,128)S(1)}, f32[4,256]{1,0:T(4,128)}, u32[]{:S(2)}) copy-start(f32[4,256]{1,0:T(4,128)} %get-tuple-element.6) | copy-start | bytes 12292
  53.9 0.7 %copy-start.1 = (f32[4,128]{1,0:T(4,128)S(1)}, f32[4,128]{1,0:T(4,128)}, u32[]{:S(2)}) copy-start(f32[4,128]{1,0:T(4,128)} %get-tuple-element.7) | copy-start | bytes 6148
  54.6 0.7 %copy-start.2 = (f32[2,64]{1,0:T(2,128)S(1)}, f32[2,64]{1,0:T(2,128)}, u32[]{:S(2)}) copy-start(f32[2,64]{1,0:T(2,128)} %get-tuple-element.8) | copy-start | bytes 1540

commit v3 on v2

--- a/solution.py
+++ b/solution.py
@@ -56,12 +56,12 @@
 
 def refine_kernel(
     piece, img_h, ctf_h, cls_h, blk_h, kind_h, bank_h, fx_h, fy_h,
-    data, weight, post_out,
+    out,
     img, ctf, cls, blk, kind, bank, fx, fy, own_sem,
-    full, table, parts, rows, rid_v, rid, left, right,
+    full, inter, table, parts, rows, rid_v, rid, left, right,
     proj, cross, hist, gather_s, gather_r,
     sums, near, s1, a1, b1, s2a, s2b, a2, b2, s3, r3,
-    near_s, near_r, xs, xr, ys, yr, x2s, x2r, y2s, y2r, zs, zr,
+    near_s, near_r, xs, xr, ys, yr, x2s, x2r, y2s, y2r, zs, zr, here,
 ):
     p = lax.axis_index("particle")
     s = lax.axis_index("slab")
@@ -95,7 +95,7 @@
         copy.start()
         return copy
 
-    peers = [sibling] + [x_peer(d)[1] for d in (1, 2, 3)] + [z_peer(d)[1] for d in range(1, 8)]
+    peers = [sibling] + [x_peer(d)[1] for d in (1, 2, 3)] + [z_peer(d)[1] for d in (1, 7)]
     peers += [map_peer(d) for d in range(1, 8)]
     barrier = pltpu.get_barrier_semaphore()
     for peer in peers:
@@ -112,12 +112,22 @@
     for d in (6, 2, 5, 3, 7, 1, 4):
         sends.append(send(piece, full.at[s], gather_s.at[d], gather_r.at[d], map_peer(d)))
 
+    def tell(n):
+        for side, d in enumerate((1, 7)):
+            pl.semaphore_signal(here.at[n, side], inc=1, device_id=z_peer(d)[1], device_id_type=MESH)
+
+    def hear(n):
+        for side in range(2):
+            pl.semaphore_wait(here.at[n, side], 1)
+
+    tell(0)
+
     loads[0].wait()
     loads[1].wait()
     number = kind[...] * NBLK + blk[...]
     for h in range(2):
         pair = jnp.concatenate([number[:, 2 * h, :], number[:, 2 * h + 1, :]], axis=1)
-        rid_v[pl.ds(h * 32, 32), :] = pair
+        rid_v[pl.ds(h * 32, 32), :] = pair * 2
     to_scalar = pltpu.make_async_copy(rid_v, rid, own_sem.at[len(pairs)])
     to_scalar.start()
 
@@ -136,10 +146,10 @@
                 parts[pl.ds(c * 32 + i * PB + b, 1), :] = row[:, b * BW : (b + 1) * BW]
     both = jnp.concatenate(split(parts[...]), axis=0)
     for k in range(KINDS):
-        out = lax.dot_general(both, bank[k], NT, preferred_element_type=F32)
-        out = out[:96] + out[96:]
+        turned = lax.dot_general(both, bank[k], NT, preferred_element_type=F32)
+        turned = turned[:96] + turned[96:]
         for c in range(3):
-            rows[c, pl.ds(k, 32, stride=KINDS), :] = out[c * 32 : (c + 1) * 32]
+            rows[c, pl.ds(k, 32, stride=KINDS), :] = turned[c * 32 : (c + 1) * 32]
 
     row_id = lax.broadcasted_iota(jnp.int32, (64, 128), 0)
     col_id = lax.broadcasted_iota(jnp.int32, (128, 128), 0)
@@ -147,22 +157,25 @@
     @pl.loop(0, 32)
     def _(ip):
         for h in range(2):
-            v = rid_v[pl.ds(h * 32 + ip, 1), :]
+            v = rid_v[pl.ds(h * 32 + ip, 1), :] >> 1
             high = ((v >> 5) & 1) * 4 + ((v >> 4) & 1) * 2 + ((v >> 6) & 1)
             low = ((v >> 2) & 3) * 32 + ((v >> 7) & 7) * 4 + (v & 3)
             at = pl.ds(h * 128, 128)
             left[ip, :, at] = jnp.where(row_id == high * KINDS + (v >> 10), 1.0, 0.0).astype(BF16)
             right[ip, :, at] = jnp.where(col_id == low, 1.0, 0.0).astype(BF16)
 
+    hear(0)
+    tell(1)
+
     def map_piece(source):
-        lhs = jnp.concatenate([full[source, :, :BW], full[source, :, BW:]], axis=0)
+        inter[pl.ds(0, BW, stride=2), :] = full[source, :, :BW].astype(F32)
+        inter[pl.ds(1, BW, stride=2), :] = full[source, :, BW:].astype(F32)
+        lhs = inter[...].astype(BF16)
         for k in range(0, KINDS, 2):
-            out = jnp.dot(lhs, jnp.concatenate([bank[k], bank[k + 1]], axis=1), preferred_element_type=F32)
+            mapped = jnp.dot(lhs, jnp.concatenate([bank[k], bank[k + 1]], axis=1), preferred_element_type=F32)
             for h in range(2):
-                at = pl.ds(pl.multiple_of((k + h) * NBLK + source * BW, BW), BW)
-                for c in range(2):
-                    half = out[c * BW : (c + 1) * BW, h * BW : (h + 1) * BW]
-                    table[c, at, :] = half.astype(BF16).astype(F32)
+                at = pl.ds(pl.multiple_of((k + h) * 2 * NBLK + source * 256, 256), 256)
+                table[at, :] = mapped[:, h * BW : (h + 1) * BW].astype(BF16).astype(F32)
 
     loads[6].wait()
     map_piece(s)
@@ -176,6 +189,8 @@
         ).wait_recv()
         map_piece(source)
 
+    hear(1)
+    tell(2)
     to_scalar.wait()
     loads[7].wait()
     loads[8].wait()
@@ -185,7 +200,7 @@
         for j in range(CAND):
             taps = [rid[h * 32 + ip, q * CAND + j] for h in range(2) for q in range(2)]
             for c in range(2):
-                taken = [table[c, r] for r in taps]
+                taken = [table[r + c] for r in taps]
                 total = (taken[0] + taken[1]) + (taken[2] + taken[3])
                 proj[c, pl.ds(pl.multiple_of(b * CAND, CAND) + j, 1), :] = total.reshape(1, BW)
 
@@ -207,7 +222,7 @@
         scores = scores[:, :CAND] + scores[:, CAND:]
         energy = jnp.sum(scores * scores, axis=0, keepdims=True) * (1.0 / (SIDE * SIDE))
         post = CAND * energy / (jnp.sum(energy, axis=1, keepdims=True) + 1e-6)
-        post_out[pl.ds(i, 1), :] = post
+        out[pl.ds(4 + i, 1), pl.ds(0, CAND)] = post
         pair = jnp.concatenate([post, post, post, post], axis=1)
         return split(pair)
 
@@ -215,17 +230,18 @@
         ip = i * PB + b
         hit = left[ip]
         hits = jnp.concatenate([hit * w_hi, hit * w_lo], axis=0)
-        out = lax.dot_general(hits, right[ip], NT, preferred_element_type=F32)
-        out = out[:64] + out[64:]
+        both = lax.dot_general(hits, right[ip], NT, preferred_element_type=F32)
+        both = both[:64] + both[64:]
         at = pl.ds(pl.multiple_of(ip * KINDS, KINDS), KINDS)
         for h in range(8):
-            hist[at, pl.ds(h * 128, 128)] = out[h * 8 : (h + 1) * 8]
+            hist[at, pl.ds(h * 128, 128)] = both[h * 8 : (h + 1) * 8]
 
     @pl.loop(0, PB)
     def _(b):
         gather(0, b)
 
     first = posterior(0)
+    hear(2)
 
     @pl.loop(0, PB)
     def _(b):
@@ -234,7 +250,7 @@
 
     second = posterior(1)
 
-    @pl.loop(0, PB)
+    @pl.loop(0, PB, unroll=4)
     def _(b):
         histogram(1, b, *second)
 
@@ -244,9 +260,9 @@
     def map_sums(of_core, to):
         start = pl.multiple_of((of_core * 4 + to) * 128, 128)
         h_hi, h_lo = split(hist[:, pl.ds(start, 128)].T)
-        out = jnp.dot(h_hi, d_both, preferred_element_type=F32)
-        out = out[:, :384] + out[:, 384:] + jnp.dot(h_lo, d_hi, preferred_element_type=F32)
-        return out.reshape(4, 32, 384)
+        got = jnp.dot(h_hi, d_both, preferred_element_type=F32)
+        got = got[:, :384] + got[:, 384:] + jnp.dot(h_lo, d_hi, preferred_element_type=F32)
+        return got.reshape(4, 32, 384)
 
     order = (2, 1, 3, 0)
     to_near = []
@@ -298,8 +314,7 @@
     total = s3[z]
     for d in range(1, 8):
         total = total + r3[d]
-    data[...] = total[:, :256]
-    weight[...] = total[:, 256:]
+    out[0:4, :] = total
     for copy in sends + to_near + last + done + then + third:
         copy.wait_send()
 
@@ -309,15 +324,11 @@
     kind = jnp.transpose(interp_kind, (0, 2, 3, 1)).reshape(32, TAPS, CAND)
     dma = pltpu.SemaphoreType.DMA
     i32 = jnp.int32
-    return pl.pallas_call(
+    out = pl.pallas_call(
         refine_kernel,
-        out_shape=[
-            jax.ShapeDtypeStruct((4, 256), F32),
-            jax.ShapeDtypeStruct((4, 128), F32),
-            jax.ShapeDtypeStruct((2, CAND), F32),
-        ],
+        out_shape=jax.ShapeDtypeStruct((8, 384), F32),
         in_specs=[pl.BlockSpec(memory_space=pltpu.HBM)] * 9,
-        out_specs=[pl.BlockSpec(memory_space=VMEM)] * 3,
+        out_specs=pl.BlockSpec(memory_space=VMEM),
         scratch_shapes=[
             VMEM((2, 2, 2048), BF16),
             VMEM((64, 2048), BF16),
@@ -329,7 +340,8 @@
             VMEM((1024, 512), BF16),
             dma((10,)),
             VMEM((8, BW, 2 * BW), BF16),
-            VMEM((2, KINDS * NBLK, BW), F32),
+            VMEM((2 * BW, BW), F32),
+            VMEM((2 * KINDS * NBLK, BW), F32),
             VMEM((96, BW), F32),
             VMEM((3, 256, BW), F32),
             VMEM((64, 128), i32),
@@ -353,6 +365,7 @@
             VMEM((8, 4, 384), F32),
             dma((4,)), dma((4,)), dma((4,)), dma((4,)), dma((4,)), dma((4,)),
             dma((4,)), dma((4,)), dma((4,)), dma((4,)), dma((8,)), dma((8,)),
+            pltpu.SemaphoreType.REGULAR((3, 2)),
         ],
         compiler_params=pltpu.CompilerParams(
             collective_id=0, has_side_effects=True, vmem_limit_bytes=56 * 1024 * 1024
@@ -362,6 +375,7 @@
         ref_map, images, ctf_table, ctf_class, blk, kind, interp_bank,
         jnp.asarray(line_table(), BF16), jnp.asarray(across_table(), BF16),
     )
+    return (out[:4, :256], out[:4, 256:], out[4:6, :CAND])
 
 
 def solution(mesh):

time: 56.5 us -> 54.7 us (0.968)
  Pallas kernels: 52.6 us -> 49.5 us
  local copies, waits for them, and re-layouts: 2.56 us -> 3.79 us
    slice x0 -> x3, local copies, waits for them, and re-layouts: none -> 3.79 us  [local(): return (out[:4, :256], out[:4, 256:], out[4:6, :CAND])]
    pallas_call x1, Pallas kernels: 52.6 us -> 49.5 us  [local(): pl.pallas_call(refine_kernel, out_shape=jax.ShapeDtypeStruct((8, 384), F3...]
    unnamed x9 -> x0, local copies, waits for them, and re-layouts: 2.56 us -> none
where the time goes in v3:
time: 54.7 us; the launch traced here: 53.9 us
  Pallas kernels  49.5 us (90%)
  local copies, waits for them, and re-layouts  3.79 us (7%)
  between operations  0.64 us (1%)
    pallas_call x1, Pallas kernels, local(): pl.pallas_call(refine_kernel, out_shape=jax.ShapeDtypeStruct((8, 384), F3...  49.5 us
    slice x3, local copies, waits for them, and re-layouts, local(): return (out[:4, :256], out[:4, 256:], out[4:6, :CAND])  3.79 us

profile of v3, /device:TPU:1, one launch (start us, length us, event | category | flops | bytes accessed | tf_op | source)
XLA Modules:
  0.0 53.9 jit_solution(8234079460789263706)
XLA Ops:
  0.6 49.5 %refine.1 = f32[8,384]{1,0:T(8,128)} custom-call(bf16[128,256]{1,0:T(8,128)(2,1)} %piece.1, bf16[2,2,2048]{2,1,0:T(2,128)(2,1)} %img_h.1, bf16[64,2048]{1,0:T(8,128)(2,1)} %ctf_h.1, s32[2]{0:T(128)} %cls_h.1, s32[32,4,64]{2,1,0:T(4,128)} %bitcast.6, s32[32,4,64]{2,1,0:T(4,128)} %bitcast.7, bf16[8,128,128]{2,1,0:T(8,128)(2,1)} %bank_h.1, ...), custom_call_target="tpu_custom_call" | custom-call | tf_op jit(solution)/shard_map/refine/pallas_call | solution.py:327
  50.1 1.2 %slice.11 = f32[2,64]{1,0:T(2,128)} slice(f32[8,384]{1,0:T(8,128)} %refine.1), slice={[4:6], [0:64]} | slice | bytes 1024 | tf_op jit(solution)/shard_map/slice | solution.py:378
  51.4 1.3 %slice.10 = f32[4,128]{1,0:T(4,128)} slice(f32[8,384]{1,0:T(8,128)} %refine.1), slice={[0:4], [256:384]} | slice | bytes 4096 | tf_op jit(solution)/shard_map/slice | solution.py:378
  52.6 1.3 %slice.9 = f32[4,256]{1,0:T(4,128)} slice(f32[8,384]{1,0:T(8,128)} %refine.1), slice={[0:4], [0:256]} | slice | bytes 8192 | tf_op jit(solution)/shard_map/slice | solution.py:378

commit v4 on v3

--- a/solution.py
+++ b/solution.py
@@ -16,6 +16,7 @@
 PB = 16
 NBLK = 1024
 MESH = pl.DeviceIdType.MESH
+ORDER = (1, 2, 3, 4, 5, 6, 7)
 VMEM = pltpu.VMEM
 F32 = jnp.float32
 BF16 = jnp.bfloat16
@@ -56,10 +57,10 @@
 
 def refine_kernel(
     piece, img_h, ctf_h, cls_h, blk_h, kind_h, bank_h, fx_h, fy_h,
-    out,
+    data, weight, post_out,
     img, ctf, cls, blk, kind, bank, fx, fy, own_sem,
     full, inter, table, parts, rows, rid_v, rid, left, right,
-    proj, cross, hist, gather_s, gather_r,
+    proj, cross, hist, gather_s, gather_r, forward_s, forward_r,
     sums, near, s1, a1, b1, s2a, s2b, a2, b2, s3, r3,
     near_s, near_r, xs, xr, ys, yr, x2s, x2r, y2s, y2r, zs, zr, here,
 ):
@@ -83,10 +84,10 @@
         to = lax.rem(z + d, 8)
         return to, (p + (to - z) * 4, s)
 
-    def map_peer(d):
-        other = lax.rem(s + d, 8)
-        apart = other // 4 - x_hi
-        return (p + apart * apart * (2 - 4 * x_lo), other)
+    def map_peer(n, sign):
+        flip = lax.rem(n, 2)
+        to = lax.rem(y + 4 + sign * (n // 2), 4)
+        return (p + flip * (2 - 4 * x_lo), (x_hi + flip * (1 - 2 * x_hi)) * 4 + to)
 
     def send(src, dst, ssem, rsem, peer):
         copy = pltpu.make_async_remote_copy(
@@ -96,7 +97,7 @@
         return copy
 
     peers = [sibling] + [x_peer(d)[1] for d in (1, 2, 3)] + [z_peer(d)[1] for d in (1, 7)]
-    peers += [map_peer(d) for d in range(1, 8)]
+    peers += [map_peer(n, 1) for n in range(1, 8)]
     barrier = pltpu.get_barrier_semaphore()
     for peer in peers:
         pl.semaphore_signal(barrier, inc=1, device_id=peer, device_id_type=MESH)
@@ -108,9 +109,10 @@
     for load in loads:
         load.start()
     pl.semaphore_wait(barrier, len(peers))
+    half = pl.ds(pl.multiple_of(core * 64, 64), 64)
     sends = []
-    for d in (6, 2, 5, 3, 7, 1, 4):
-        sends.append(send(piece, full.at[s], gather_s.at[d], gather_r.at[d], map_peer(d)))
+    for n in ORDER:
+        sends.append(send(piece.at[half], full.at[s, half], gather_s.at[n], gather_r.at[n], map_peer(n, 1)))
 
     def tell(n):
         for side, d in enumerate((1, 7)):
@@ -164,9 +166,6 @@
             left[ip, :, at] = jnp.where(row_id == high * KINDS + (v >> 10), 1.0, 0.0).astype(BF16)
             right[ip, :, at] = jnp.where(col_id == low, 1.0, 0.0).astype(BF16)
 
-    hear(0)
-    tell(1)
-
     def map_piece(source):
         inter[pl.ds(0, BW, stride=2), :] = full[source, :, :BW].astype(F32)
         inter[pl.ds(1, BW, stride=2), :] = full[source, :, BW:].astype(F32)
@@ -180,17 +179,32 @@
     loads[6].wait()
     map_piece(s)
 
+    def forward(n, rows):
+        at = full.at[map_peer(n, -1)[1], rows]
+        return pltpu.make_async_remote_copy(
+            src_ref=at, dst_ref=at, send_sem=forward_s.at[n], recv_sem=forward_r.at[n],
+            device_id=sibling, device_id_type=MESH,
+        )
+
+    other_half = pl.ds(pl.multiple_of((1 - core) * 64, 64), 64)
+    for n in ORDER:
+        peer = map_peer(n, -1)
+        pltpu.make_async_remote_copy(
+            src_ref=piece.at[half], dst_ref=full.at[peer[1], half], send_sem=gather_s.at[n],
+            recv_sem=gather_r.at[n], device_id=peer, device_id_type=MESH,
+        ).wait_recv()
+        forward(n, half).start()
+
     @pl.loop(1, 8)
-    def _(d):
-        source = lax.rem(s + 8 - d, 8)
-        pltpu.make_async_remote_copy(
-            src_ref=piece, dst_ref=full.at[source], send_sem=gather_s.at[d], recv_sem=gather_r.at[d],
-            device_id=map_peer(d), device_id_type=MESH,
-        ).wait_recv()
-        map_piece(source)
-
-    hear(1)
-    tell(2)
+    def _(n):
+        forward(n, other_half).wait_recv()
+        map_piece(map_peer(n, -1)[1])
+
+    for n in range(1, 8):
+        forward(n, half).wait_send()
+
+    hear(0)
+    tell(1)
     to_scalar.wait()
     loads[7].wait()
     loads[8].wait()
@@ -199,17 +213,16 @@
         ip = i * PB + b
         for j in range(CAND):
             taps = [rid[h * 32 + ip, q * CAND + j] for h in range(2) for q in range(2)]
-            for c in range(2):
-                taken = [table[r + c] for r in taps]
-                total = (taken[0] + taken[1]) + (taken[2] + taken[3])
-                proj[c, pl.ds(pl.multiple_of(b * CAND, CAND) + j, 1), :] = total.reshape(1, BW)
+            taken = [table[pl.ds(r, 2), :] for r in taps]
+            total = (taken[0] + taken[1]) + (taken[2] + taken[3])
+            proj[pl.ds(pl.multiple_of(b * 2 * CAND, 2 * CAND) + 2 * j, 2), :] = total
 
     def posterior(i):
         for b in range(PB):
             ca = parts[pl.ds(i * PB + b, 1), :]
             cb = parts[pl.ds(32 + i * PB + b, 1), :]
-            u = proj[0, pl.ds(b * CAND, CAND), :]
-            w = proj[1, pl.ds(b * CAND, CAND), :]
+            u = proj[pl.ds(b * 2 * CAND, CAND, stride=2), :]
+            w = proj[pl.ds(b * 2 * CAND + 1, CAND, stride=2), :]
             cross[:, pl.ds(b * 256, 128)] = (ca * u + cb * w).astype(BF16)
             cross[:, pl.ds(b * 256 + 128, 128)] = (cb * u - ca * w).astype(BF16)
         along = [
@@ -222,7 +235,7 @@
         scores = scores[:, :CAND] + scores[:, CAND:]
         energy = jnp.sum(scores * scores, axis=0, keepdims=True) * (1.0 / (SIDE * SIDE))
         post = CAND * energy / (jnp.sum(energy, axis=1, keepdims=True) + 1e-6)
-        out[pl.ds(4 + i, 1), pl.ds(0, CAND)] = post
+        post_out[pl.ds(i, 1), :] = post
         pair = jnp.concatenate([post, post, post, post], axis=1)
         return split(pair)
 
@@ -241,18 +254,21 @@
         gather(0, b)
 
     first = posterior(0)
-    hear(2)
+    hear(1)
+    tell(2)
 
     @pl.loop(0, PB)
     def _(b):
         gather(1, b)
-        histogram(0, b, *first)
 
     second = posterior(1)
-
-    @pl.loop(0, PB, unroll=4)
-    def _(b):
-        histogram(1, b, *second)
+    hear(2)
+
+    for i, pair in enumerate((first, second)):
+
+        @pl.loop(0, PB, unroll=8)
+        def _(b):
+            histogram(i, b, *pair)
 
     d_hi, d_lo = split(jnp.concatenate([rows[c] for c in range(3)], axis=1))
     d_both = jnp.concatenate([d_hi, d_lo], axis=1)
@@ -314,7 +330,8 @@
     total = s3[z]
     for d in range(1, 8):
         total = total + r3[d]
-    out[0:4, :] = total
+    data[...] = total[:, :256]
+    weight[...] = total[:, 256:]
     for copy in sends + to_near + last + done + then + third:
         copy.wait_send()
 
@@ -324,11 +341,15 @@
     kind = jnp.transpose(interp_kind, (0, 2, 3, 1)).reshape(32, TAPS, CAND)
     dma = pltpu.SemaphoreType.DMA
     i32 = jnp.int32
-    out = pl.pallas_call(
+    return pl.pallas_call(
         refine_kernel,
-        out_shape=jax.ShapeDtypeStruct((8, 384), F32),
+        out_shape=[
+            jax.ShapeDtypeStruct((4, 256), F32),
+            jax.ShapeDtypeStruct((4, 128), F32),
+            jax.ShapeDtypeStruct((2, CAND), F32),
+        ],
         in_specs=[pl.BlockSpec(memory_space=pltpu.HBM)] * 9,
-        out_specs=pl.BlockSpec(memory_space=VMEM),
+        out_specs=[pl.BlockSpec(memory_space=VMEM)] * 3,
         scratch_shapes=[
             VMEM((2, 2, 2048), BF16),
             VMEM((64, 2048), BF16),
@@ -348,10 +369,10 @@
             pltpu.SMEM((64, 128), i32),
             VMEM((32, 64, 256), BF16),
             VMEM((32, 128, 256), BF16),
-            VMEM((2, CAND * PB, BW), F32),
+            VMEM((2 * CAND * PB, BW), F32),
             VMEM((CAND, 4096), BF16),
             VMEM((256, NBLK), F32),
-            dma((8,)), dma((8,)),
+            dma((8,)), dma((8,)), dma((8,)), dma((8,)),
             VMEM((4, 4, 32, 384), F32),
             VMEM((4, 4, 32, 384), F32),
             VMEM((4, 4, 32, 384), F32),
@@ -375,7 +396,6 @@
         ref_map, images, ctf_table, ctf_class, blk, kind, interp_bank,
         jnp.asarray(line_table(), BF16), jnp.asarray(across_table(), BF16),
     )
-    return (out[:4, :256], out[:4, 256:], out[4:6, :CAND])
 
 
 def solution(mesh):

time: 54.7 us -> 50 us (0.914); the launches traced: 53.9 us -> 49.8 us
  Pallas kernels: 49.5 us -> 46.6 us
  local copies, waits for them, and re-layouts: 3.79 us -> 2.56 us
    slice x3 -> x0, local copies, waits for them, and re-layouts: 3.79 us -> none  [local(): return (out[:4, :256], out[:4, 256:], out[4:6, :CAND])]
    pallas_call x1, Pallas kernels: 49.5 us -> 46.6 us  [local(): pl.pallas_call(refine_kernel, out_shape=[jax.ShapeDtypeStruct((4, 256), F...]
    unnamed x0 -> x9, local copies, waits for them, and re-layouts: none -> 2.56 us
where the time goes in v4:
time: 50 us; the launch traced here: 49.8 us
  Pallas kernels  46.6 us (93%)
  local copies, waits for them, and re-layouts  2.56 us (5%)
  between operations  0.65 us (1%)
    pallas_call x1, Pallas kernels, local(): pl.pallas_call(refine_kernel, out_shape=[jax.ShapeDtypeStruct((4, 256), F...  46.6 us
    unnamed x9, local copies, waits for them, and re-layouts  2.56 us

profile of v4, /device:TPU:1, one launch (start us, length us, event | category | flops | bytes accessed | tf_op | source)
XLA Modules:
  0.0 49.8 jit_solution(2483756599865127438)
XLA Ops:
  0.6 46.6 %refine.1 = (f32[4,256]{1,0:T(4,128)}, f32[4,128]{1,0:T(4,128)}, f32[2,64]{1,0:T(2,128)}) custom-call(bf16[128,256]{1,0:T(8,128)(2,1)} %piece.1, bf16[2,2,2048]{2,1,0:T(2,128)(2,1)} %img_h.1, bf16[64,2048]{1,0:T(8,128)(2,1)} %ctf_h.1, s32[2]{0:T(128)} %cls_h.1, s32[32,4,64]{2,1,0:T(4,128)} %bitcast.6, s32[32,4,64]{2,1,0:T(4,128)} %bitcast.7, ...), custom_call_target="tpu_custom_call" | custom-call | tf_op jit(solution)/shard_map/refine/pallas_call | solution.py:344
  47.2 0.0 copy-start
  47.2 0.7 %copy-done = f32[4,256]{1,0:T(4,128)S(1)} copy-done((f32[4,256]{1,0:T(4,128)S(1)}, f32[4,256]{1,0:T(4,128)}, u32[]{:S(2)}) %copy-start) | copy-done | bytes 4120
  47.9 0.0 copy-start.1
  47.9 0.6 %copy.15 = f32[4,256]{1,0:T(4,128)} copy(f32[4,256]{1,0:T(4,128)S(1)} %copy-done) | data formatting | bytes 8192
  48.5 0.1 copy-done.1
  48.6 0.0 copy-start.2
  48.6 0.6 %copy.16 = f32[4,128]{1,0:T(4,128)} copy(f32[4,128]{1,0:T(4,128)S(1)} %copy-done.1) | data formatting | bytes 4096
  49.2 0.1 copy-done.2
  49.2 0.6 %copy.17 = f32[2,64]{1,0:T(2,128)} copy(f32[2,64]{1,0:T(2,128)S(1)} %copy-done.2) | data formatting | bytes 1024
Async XLA Ops:
  47.2 0.7 %copy-start = (f32[4,256]{1,0:T(4,128)S(1)}, f32[4,256]{1,0:T(4,128)}, u32[]{:S(2)}) copy-start(f32[4,256]{1,0:T(4,128)} %get-tuple-element.6) | copy-start | bytes 12292
  47.9 0.7 %copy-start.1 = (f32[4,128]{1,0:T(4,128)S(1)}, f32[4,128]{1,0:T(4,128)}, u32[]{:S(2)}) copy-start(f32[4,128]{1,0:T(4,128)} %get-tuple-element.7) | copy-start | bytes 6148
  48.6 0.7 %copy-start.2 = (f32[2,64]{1,0:T(2,128)S(1)}, f32[2,64]{1,0:T(2,128)}, u32[]{:S(2)}) copy-start(f32[2,64]{1,0:T(2,128)} %get-tuple-element.8) | copy-start | bytes 1540

commit v5 on v4

--- a/solution.py
+++ b/solution.py
@@ -16,6 +16,7 @@
 PB = 16
 NBLK = 1024
 MESH = pl.DeviceIdType.MESH
+SLOTS = 4
 ORDER = (1, 2, 3, 4, 5, 6, 7)
 VMEM = pltpu.VMEM
 F32 = jnp.float32
@@ -59,7 +60,7 @@
     piece, img_h, ctf_h, cls_h, blk_h, kind_h, bank_h, fx_h, fy_h,
     data, weight, post_out,
     img, ctf, cls, blk, kind, bank, fx, fy, own_sem,
-    full, inter, table, parts, rows, rid_v, rid, left, right,
+    full, inter, table, parts, rows, rid_v, rids, rid_s, left, right,
     proj, cross, hist, gather_s, gather_r, forward_s, forward_r,
     sums, near, s1, a1, b1, s2a, s2b, a2, b2, s3, r3,
     near_s, near_r, xs, xr, ys, yr, x2s, x2r, y2s, y2r, zs, zr, here,
@@ -129,9 +130,13 @@
     number = kind[...] * NBLK + blk[...]
     for h in range(2):
         pair = jnp.concatenate([number[:, 2 * h, :], number[:, 2 * h + 1, :]], axis=1)
-        rid_v[pl.ds(h * 32, 32), :] = pair * 2
-    to_scalar = pltpu.make_async_copy(rid_v, rid, own_sem.at[len(pairs)])
-    to_scalar.start()
+        rid_v[:, h, :] = pair * 2
+
+    def fetch(u, ip):
+        return pltpu.make_async_copy(rid_v.at[ip], rids[u], rid_s.at[u])
+
+    for u in range(SLOTS):
+        fetch(u, u).start()
 
     for load in loads[2:6]:
         load.wait()
@@ -159,7 +164,7 @@
     @pl.loop(0, 32)
     def _(ip):
         for h in range(2):
-            v = rid_v[pl.ds(h * 32 + ip, 1), :] >> 1
+            v = rid_v[ip, pl.ds(h, 1), :] >> 1
             high = ((v >> 5) & 1) * 4 + ((v >> 4) & 1) * 2 + ((v >> 6) & 1)
             low = ((v >> 2) & 3) * 32 + ((v >> 7) & 7) * 4 + (v & 3)
             at = pl.ds(h * 128, 128)
@@ -187,7 +192,7 @@
         )
 
     other_half = pl.ds(pl.multiple_of((1 - core) * 64, 64), 64)
-    for n in ORDER:
+    def pass_on(n):
         peer = map_peer(n, -1)
         pltpu.make_async_remote_copy(
             src_ref=piece.at[half], dst_ref=full.at[peer[1], half], send_sem=gather_s.at[n],
@@ -195,49 +200,60 @@
         ).wait_recv()
         forward(n, half).start()
 
-    @pl.loop(1, 8)
-    def _(n):
+    def use(n):
         forward(n, other_half).wait_recv()
         map_piece(map_peer(n, -1)[1])
 
+    pass_on(1)
+
+    @pl.loop(1, 7)
+    def _(n):
+        pass_on(n + 1)
+        use(n)
+
+    use(7)
     for n in range(1, 8):
         forward(n, half).wait_send()
 
     hear(0)
     tell(1)
-    to_scalar.wait()
     loads[7].wait()
     loads[8].wait()
 
-    def gather(i, b):
-        ip = i * PB + b
-        for j in range(CAND):
-            taps = [rid[h * 32 + ip, q * CAND + j] for h in range(2) for q in range(2)]
-            taken = [table[pl.ds(r, 2), :] for r in taps]
-            total = (taken[0] + taken[1]) + (taken[2] + taken[3])
-            proj[pl.ds(pl.multiple_of(b * 2 * CAND, 2 * CAND) + 2 * j, 2), :] = total
-
-    def posterior(i):
+    @pl.loop(0, 2)
+    def _(i):
+        @pl.loop(0, PB // SLOTS)
+        def _(g):
+            for u in range(SLOTS):
+                b = g * SLOTS + u
+                ip = i * PB + b
+                fetch(u, ip).wait()
+                for j in range(CAND):
+                    taken = [table[pl.ds(rids[u][h, q * CAND + j], 2), :] for h in range(2) for q in range(2)]
+                    total = (taken[0] + taken[1]) + (taken[2] + taken[3])
+                    proj[pl.ds(pl.multiple_of(b * 2 * CAND, 2 * CAND) + 2 * j, 2), :] = total
+                fetch(u, lax.rem(ip + SLOTS, 32)).start()
+
         for b in range(PB):
             ca = parts[pl.ds(i * PB + b, 1), :]
             cb = parts[pl.ds(32 + i * PB + b, 1), :]
             u = proj[pl.ds(b * 2 * CAND, CAND, stride=2), :]
             w = proj[pl.ds(b * 2 * CAND + 1, CAND, stride=2), :]
-            cross[:, pl.ds(b * 256, 128)] = (ca * u + cb * w).astype(BF16)
-            cross[:, pl.ds(b * 256 + 128, 128)] = (cb * u - ca * w).astype(BF16)
-        along = [
-            jnp.dot(cross[:, g * 1024 : (g + 1) * 1024], fx[...], preferred_element_type=F32)
-            for g in range(4)
-        ]
-        along = jnp.concatenate(along, axis=1)
+            at = pl.ds(b // 4 * CAND, CAND)
+            cross[at, pl.ds(b % 4 * 256, 128)] = (ca * u + cb * w).astype(BF16)
+            cross[at, pl.ds(b % 4 * 256 + 128, 128)] = (cb * u - ca * w).astype(BF16)
+        along = jnp.dot(cross[...], fx[...], preferred_element_type=F32)
+        along = jnp.concatenate([along[g * CAND : (g + 1) * CAND] for g in range(4)], axis=1)
         both = jnp.concatenate(split(along), axis=0)
         scores = lax.dot_general(fy[...], both, NT, preferred_element_type=F32)
         scores = scores[:, :CAND] + scores[:, CAND:]
         energy = jnp.sum(scores * scores, axis=0, keepdims=True) * (1.0 / (SIDE * SIDE))
-        post = CAND * energy / (jnp.sum(energy, axis=1, keepdims=True) + 1e-6)
-        post_out[pl.ds(i, 1), :] = post
-        pair = jnp.concatenate([post, post, post, post], axis=1)
-        return split(pair)
+        post_out[pl.ds(i, 1), :] = CAND * energy / (jnp.sum(energy, axis=1, keepdims=True) + 1e-6)
+
+    for u in range(SLOTS):
+        fetch(u, u).wait()
+    hear(1)
+    tell(2)
 
     def histogram(i, b, w_hi, w_lo):
         ip = i * PB + b
@@ -249,22 +265,9 @@
         for h in range(8):
             hist[at, pl.ds(h * 128, 128)] = both[h * 8 : (h + 1) * 8]
 
-    @pl.loop(0, PB)
-    def _(b):
-        gather(0, b)
-
-    first = posterior(0)
-    hear(1)
-    tell(2)
-
-    @pl.loop(0, PB)
-    def _(b):
-        gather(1, b)
-
-    second = posterior(1)
-    hear(2)
-
-    for i, pair in enumerate((first, second)):
+    for i in range(2):
+        post = post_out[pl.ds(i, 1), :]
+        pair = split(jnp.concatenate([post, post, post, post], axis=1))
 
         @pl.loop(0, PB, unroll=8)
         def _(b):
@@ -321,6 +324,7 @@
     high = (s2b[x] + b2[1]) + (b2[2] + b2[3])
     for n in range(4):
         s3[4 + n] = high[n * 4 : (n + 1) * 4]
+    hear(2)
     third = []
     for d in (4, 3, 5, 2, 6, 1, 7):
         to, peer = z_peer(d)
@@ -365,12 +369,13 @@
             VMEM((2 * KINDS * NBLK, BW), F32),
             VMEM((96, BW), F32),
             VMEM((3, 256, BW), F32),
-            VMEM((64, 128), i32),
-            pltpu.SMEM((64, 128), i32),
+            VMEM((32, 2, 128), i32),
+            [pltpu.SMEM((2, 128), i32)] * SLOTS,
+            dma((SLOTS,)),
             VMEM((32, 64, 256), BF16),
             VMEM((32, 128, 256), BF16),
             VMEM((2 * CAND * PB, BW), F32),
-            VMEM((CAND, 4096), BF16),
+            VMEM((4 * CAND, 1024), BF16),
             VMEM((256, NBLK), F32),
             dma((8,)), dma((8,)), dma((8,)), dma((8,)),
             VMEM((4, 4, 32, 384), F32),

time: 50 us -> 48.9 us (0.978)
  Pallas kernels: 46.6 us -> 45.4 us
    pallas_call x1, Pallas kernels: 46.6 us -> 45.4 us  [local(): pl.pallas_call(refine_kernel, out_shape=[jax.ShapeDtypeStruct((4, 256), F...]
where the time goes in v5:
time: 48.9 us; the launch traced here: 48.6 us
  Pallas kernels  45.4 us (93%)
  local copies, waits for them, and re-layouts  2.56 us (5%)
  between operations  0.65 us (1%)
    pallas_call x1, Pallas kernels, local(): pl.pallas_call(refine_kernel, out_shape=[jax.ShapeDtypeStruct((4, 256), F...  45.4 us
    unnamed x9, local copies, waits for them, and re-layouts  2.56 us

profile of v5, /device:TPU:1, one launch (start us, length us, event | category | flops | bytes accessed | tf_op | source)
XLA Modules:
  0.0 48.6 jit_solution(16547868750755207161)
XLA Ops:
  0.6 45.4 %refine.1 = (f32[4,256]{1,0:T(4,128)}, f32[4,128]{1,0:T(4,128)}, f32[2,64]{1,0:T(2,128)}) custom-call(bf16[128,256]{1,0:T(8,128)(2,1)} %piece.1, bf16[2,2,2048]{2,1,0:T(2,128)(2,1)} %img_h.1, bf16[64,2048]{1,0:T(8,128)(2,1)} %ctf_h.1, s32[2]{0:T(128)} %cls_h.1, s32[32,4,64]{2,1,0:T(4,128)} %bitcast.6, s32[32,4,64]{2,1,0:T(4,128)} %bitcast.7, ...), custom_call_target="tpu_custom_call" | custom-call | tf_op jit(solution)/shard_map/refine/pallas_call | solution.py:348
  46.0 0.0 copy-start
  46.0 0.7 %copy-done = f32[4,256]{1,0:T(4,128)S(1)} copy-done((f32[4,256]{1,0:T(4,128)S(1)}, f32[4,256]{1,0:T(4,128)}, u32[]{:S(2)}) %copy-start) | copy-done | bytes 4120
  46.7 0.0 copy-start.1
  46.7 0.6 %copy.15 = f32[4,256]{1,0:T(4,128)} copy(f32[4,256]{1,0:T(4,128)S(1)} %copy-done) | data formatting | bytes 8192
  47.3 0.1 copy-done.1
  47.4 0.0 copy-start.2
  47.4 0.6 %copy.16 = f32[4,128]{1,0:T(4,128)} copy(f32[4,128]{1,0:T(4,128)S(1)} %copy-done.1) | data formatting | bytes 4096
  48.0 0.1 copy-done.2
  48.0 0.6 %copy.17 = f32[2,64]{1,0:T(2,128)} copy(f32[2,64]{1,0:T(2,128)S(1)} %copy-done.2) | data formatting | bytes 1024
Async XLA Ops:
  46.0 0.7 %copy-start = (f32[4,256]{1,0:T(4,128)S(1)}, f32[4,256]{1,0:T(4,128)}, u32[]{:S(2)}) copy-start(f32[4,256]{1,0:T(4,128)} %get-tuple-element.6) | copy-start | bytes 12292
  46.7 0.7 %copy-start.1 = (f32[4,128]{1,0:T(4,128)S(1)}, f32[4,128]{1,0:T(4,128)}, u32[]{:S(2)}) copy-start(f32[4,128]{1,0:T(4,128)} %get-tuple-element.7) | copy-start | bytes 6148
  47.4 0.7 %copy-start.2 = (f32[2,64]{1,0:T(2,128)S(1)}, f32[2,64]{1,0:T(2,128)}, u32[]{:S(2)}) copy-start(f32[2,64]{1,0:T(2,128)} %get-tuple-element.8) | copy-start | bytes 1540

commit v6 on v5

--- a/solution.py
+++ b/solution.py
@@ -132,8 +132,8 @@
         pair = jnp.concatenate([number[:, 2 * h, :], number[:, 2 * h + 1, :]], axis=1)
         rid_v[:, h, :] = pair * 2
 
-    def fetch(u, ip):
-        return pltpu.make_async_copy(rid_v.at[ip], rids[u], rid_s.at[u])
+    def fetch(u, two):
+        return pltpu.make_async_copy(rid_v.at[pl.ds(two * 2, 2)], rids[u], rid_s.at[u])
 
     for u in range(SLOTS):
         fetch(u, u).start()
@@ -220,35 +220,46 @@
     loads[7].wait()
     loads[8].wait()
 
-    @pl.loop(0, 2)
-    def _(i):
-        @pl.loop(0, PB // SLOTS)
-        def _(g):
-            for u in range(SLOTS):
-                b = g * SLOTS + u
-                ip = i * PB + b
-                fetch(u, ip).wait()
+    @pl.loop(0, 16 // SLOTS)
+    def _(step):
+        for u in range(SLOTS):
+            two = step * SLOTS + u
+            i = two // 8
+            fetch(u, two).wait()
+            for v in range(2):
+                start = (u * 2 + v) * 2 * CAND
                 for j in range(CAND):
-                    taken = [table[pl.ds(rids[u][h, q * CAND + j], 2), :] for h in range(2) for q in range(2)]
-                    total = (taken[0] + taken[1]) + (taken[2] + taken[3])
-                    proj[pl.ds(pl.multiple_of(b * 2 * CAND, 2 * CAND) + 2 * j, 2), :] = total
-                fetch(u, lax.rem(ip + SLOTS, 32)).start()
-
-        for b in range(PB):
-            ca = parts[pl.ds(i * PB + b, 1), :]
-            cb = parts[pl.ds(32 + i * PB + b, 1), :]
-            u = proj[pl.ds(b * 2 * CAND, CAND, stride=2), :]
-            w = proj[pl.ds(b * 2 * CAND + 1, CAND, stride=2), :]
-            at = pl.ds(b // 4 * CAND, CAND)
-            cross[at, pl.ds(b % 4 * 256, 128)] = (ca * u + cb * w).astype(BF16)
-            cross[at, pl.ds(b % 4 * 256 + 128, 128)] = (cb * u - ca * w).astype(BF16)
-        along = jnp.dot(cross[...], fx[...], preferred_element_type=F32)
-        along = jnp.concatenate([along[g * CAND : (g + 1) * CAND] for g in range(4)], axis=1)
-        both = jnp.concatenate(split(along), axis=0)
-        scores = lax.dot_general(fy[...], both, NT, preferred_element_type=F32)
-        scores = scores[:, :CAND] + scores[:, CAND:]
-        energy = jnp.sum(scores * scores, axis=0, keepdims=True) * (1.0 / (SIDE * SIDE))
-        post_out[pl.ds(i, 1), :] = CAND * energy / (jnp.sum(energy, axis=1, keepdims=True) + 1e-6)
+                    taken = [table[pl.ds(rids[u][v, h, q * CAND + j], 2), :] for h in range(2) for q in range(2)]
+                    proj[pl.ds(start + 2 * j, 2), :] = (taken[0] + taken[1]) + (taken[2] + taken[3])
+                ca = parts[pl.ds(two * 2 + v, 1), :]
+                cb = parts[pl.ds(32 + two * 2 + v, 1), :]
+                re = proj[pl.ds(start, CAND, stride=2), :]
+                im = proj[pl.ds(start + 1, CAND, stride=2), :]
+                group = lax.rem(two, 8) // 2
+                at = pl.ds(pl.multiple_of(group * 2 * CAND + i * CAND, CAND), CAND)
+                lane = ((u % 2) * 2 + v) * 256
+                cross[at, pl.ds(lane, 128)] = (ca * re + cb * im).astype(BF16)
+                cross[at, pl.ds(lane + 128, 128)] = (cb * re - ca * im).astype(BF16)
+            fetch(u, lax.rem(two + SLOTS, 16)).start()
+
+    along = jnp.dot(cross[...], fx[...], preferred_element_type=F32)
+    along = jnp.concatenate([along[g * 2 * CAND : (g + 1) * 2 * CAND] for g in range(4)], axis=1)
+    both = jnp.concatenate(split(along), axis=0)
+    squares = jnp.zeros((8, 2 * CAND), F32)
+    for n in range(8):
+        scores = lax.dot_general(fy[n * 128 : (n + 1) * 128, :], both, NT, preferred_element_type=F32)
+        scores = scores[:, : 2 * CAND] + scores[:, 2 * CAND :]
+        squares = squares + jnp.sum((scores * scores).reshape(16, 8, 2 * CAND), axis=0)
+    energy = jnp.sum(squares, axis=0, keepdims=True) * (1.0 / (SIDE * SIDE))
+    lane_id = lax.broadcasted_iota(jnp.int32, (1, 2 * CAND), 1)
+    first = lane_id < CAND
+    sum0 = jnp.sum(jnp.where(first, energy, 0.0), axis=1, keepdims=True)
+    sum1 = jnp.sum(jnp.where(first, 0.0, energy), axis=1, keepdims=True)
+    post = CAND * energy / (jnp.where(first, sum0, sum1) + 1e-6)
+    turned = jnp.concatenate([post[:, CAND:], post[:, :CAND]], axis=1)
+    post_out[0:1, :] = post[:, :CAND]
+    post_out[1:2, :] = turned[:, :CAND]
+    weights = (jnp.where(first, post, turned), jnp.where(first, turned, post))
 
     for u in range(SLOTS):
         fetch(u, u).wait()
@@ -266,8 +277,7 @@
             hist[at, pl.ds(h * 128, 128)] = both[h * 8 : (h + 1) * 8]
 
     for i in range(2):
-        post = post_out[pl.ds(i, 1), :]
-        pair = split(jnp.concatenate([post, post, post, post], axis=1))
+        pair = split(jnp.concatenate([weights[i], weights[i]], axis=1))
 
         @pl.loop(0, PB, unroll=8)
         def _(b):
@@ -370,12 +380,12 @@
             VMEM((96, BW), F32),
             VMEM((3, 256, BW), F32),
             VMEM((32, 2, 128), i32),
-            [pltpu.SMEM((2, 128), i32)] * SLOTS,
+            [pltpu.SMEM((2, 2, 128), i32)] * SLOTS,
             dma((SLOTS,)),
             VMEM((32, 64, 256), BF16),
             VMEM((32, 128, 256), BF16),
-            VMEM((2 * CAND * PB, BW), F32),
-            VMEM((4 * CAND, 1024), BF16),
+            VMEM((SLOTS * 4 * CAND, BW), F32),
+            VMEM((8 * CAND, 1024), BF16),
             VMEM((256, NBLK), F32),
             dma((8,)), dma((8,)), dma((8,)), dma((8,)),
             VMEM((4, 4, 32, 384), F32),

time: 48.9 us -> 48.4 us (0.990)
  Pallas kernels: 45.4 us -> 44.9 us
where the time goes in v6:
time: 48.4 us; the launch traced here: 48.1 us
  Pallas kernels  44.9 us (93%)
  local copies, waits for them, and re-layouts  2.56 us (5%)
  between operations  0.65 us (1%)
    pallas_call x1, Pallas kernels, local(): pl.pallas_call(refine_kernel, out_shape=[jax.ShapeDtypeStruct((4, 256), F...  44.9 us
    unnamed x9, local copies, waits for them, and re-layouts  2.56 us

profile of v6, /device:TPU:1, one launch (start us, length us, event | category | flops | bytes accessed | tf_op | source)
XLA Modules:
  0.0 48.1 jit_solution(3672491384422344515)
XLA Ops:
  0.6 44.9 %refine.1 = (f32[4,256]{1,0:T(4,128)}, f32[4,128]{1,0:T(4,128)}, f32[2,64]{1,0:T(2,128)}) custom-call(bf16[128,256]{1,0:T(8,128)(2,1)} %piece.1, bf16[2,2,2048]{2,1,0:T(2,128)(2,1)} %img_h.1, bf16[64,2048]{1,0:T(8,128)(2,1)} %ctf_h.1, s32[2]{0:T(128)} %cls_h.1, s32[32,4,64]{2,1,0:T(4,128)} %bitcast.6, s32[32,4,64]{2,1,0:T(4,128)} %bitcast.7, ...), custom_call_target="tpu_custom_call" | custom-call | tf_op jit(solution)/shard_map/refine/pallas_call | solution.py:358
  45.6 0.0 copy-start
  45.6 0.7 %copy-done = f32[4,256]{1,0:T(4,128)S(1)} copy-done((f32[4,256]{1,0:T(4,128)S(1)}, f32[4,256]{1,0:T(4,128)}, u32[]{:S(2)}) %copy-start) | copy-done | bytes 4120
  46.2 0.0 copy-start.1
  46.2 0.6 %copy.15 = f32[4,256]{1,0:T(4,128)} copy(f32[4,256]{1,0:T(4,128)S(1)} %copy-done) | data formatting | bytes 8192
  46.8 0.1 copy-done.1
  46.9 0.0 copy-start.2
  46.9 0.6 %copy.16 = f32[4,128]{1,0:T(4,128)} copy(f32[4,128]{1,0:T(4,128)S(1)} %copy-done.1) | data formatting | bytes 4096
  47.5 0.1 copy-done.2
  47.6 0.6 %copy.17 = f32[2,64]{1,0:T(2,128)} copy(f32[2,64]{1,0:T(2,128)S(1)} %copy-done.2) | data formatting | bytes 1024
Async XLA Ops:
  45.6 0.7 %copy-start = (f32[4,256]{1,0:T(4,128)S(1)}, f32[4,256]{1,0:T(4,128)}, u32[]{:S(2)}) copy-start(f32[4,256]{1,0:T(4,128)} %get-tuple-element.6) | copy-start | bytes 12292
  46.2 0.7 %copy-start.1 = (f32[4,128]{1,0:T(4,128)S(1)}, f32[4,128]{1,0:T(4,128)}, u32[]{:S(2)}) copy-start(f32[4,128]{1,0:T(4,128)} %get-tuple-element.7) | copy-start | bytes 6148
  46.9 0.7 %copy-start.2 = (f32[2,64]{1,0:T(2,128)S(1)}, f32[2,64]{1,0:T(2,128)}, u32[]{:S(2)}) copy-start(f32[2,64]{1,0:T(2,128)} %get-tuple-element.8) | copy-start | bytes 1540

commit v7 on v6

--- a/solution.py
+++ b/solution.py
@@ -1,3 +1,5 @@
+import math
+
 import jax
 import jax.numpy as jnp
 import numpy as np
@@ -17,6 +19,8 @@
 NBLK = 1024
 MESH = pl.DeviceIdType.MESH
 SLOTS = 4
+FLOOR = -34
+STEPS = 585
 ORDER = (1, 2, 3, 4, 5, 6, 7)
 VMEM = pltpu.VMEM
 F32 = jnp.float32
@@ -56,14 +60,26 @@
     return hi, (v - hi.astype(F32)).astype(BF16)
 
 
+def encode(v):
+    size = jnp.log(jnp.maximum(jnp.abs(v), 2.0 ** (FLOOR - 1))) * (STEPS / math.log(2.0)) - FLOOR * STEPS
+    size = jnp.maximum(size, 0.0) + 0.5
+    return jnp.where(v < 0, -size, size).astype(jnp.int32).astype(jnp.int16)
+
+
+def decode(code):
+    step = code.astype(jnp.int32).astype(F32)
+    size = jnp.exp(jnp.abs(step) * (math.log(2.0) / STEPS) + FLOOR * math.log(2.0))
+    return jnp.where(step > 0, size, jnp.where(step < 0, -size, 0.0))
+
+
 def refine_kernel(
     piece, img_h, ctf_h, cls_h, blk_h, kind_h, bank_h, fx_h, fy_h,
     data, weight, post_out,
     img, ctf, cls, blk, kind, bank, fx, fy, own_sem,
     full, inter, table, parts, rows, rid_v, rids, rid_s, left, right,
     proj, cross, hist, gather_s, gather_r, forward_s, forward_r,
-    sums, near, s1, a1, b1, s2a, s2b, a2, b2, s3, r3,
-    near_s, near_r, xs, xr, ys, yr, x2s, x2r, y2s, y2r, zs, zr, here,
+    sums, near, mine, coded, coming, s3, r3,
+    near_s, near_r, plane_s, plane_r, zs, zr, here,
 ):
     p = lax.axis_index("particle")
     s = lax.axis_index("slab")
@@ -77,9 +93,9 @@
         to = lax.rem(x + d, 4)
         return to, (p + (lax.rem(to, 2) - x_lo) * 2, s + (to // 2 - x_hi) * 4)
 
-    def y_peer(d):
-        to = lax.rem(y + d, 4)
-        return to, (p, s + to - y)
+    def plane_peer(dx, dy):
+        to_x, to_y = lax.rem(x + dx, 4), lax.rem(y + dy, 4)
+        return to_x, to_y, (p + (lax.rem(to_x, 2) - x_lo) * 2, to_x // 2 * 4 + to_y)
 
     def z_peer(d):
         to = lax.rem(z + d, 8)
@@ -299,41 +315,30 @@
         to = lax.rem(x + d, 4)
         sums[to] = map_sums(1 - core, to)
         to_near.append(send(sums.at[to], near.at[to], near_s.at[n], near_r.at[n], sibling))
-    last = []
-    for n, d in enumerate(order):
-        to, peer = x_peer(d)
-        mine = map_sums(core, to)
+    then = []
+    for n, dx in enumerate(order):
+        to = lax.rem(x + dx, 4)
+        total = map_sums(core, to)
         to_near[n].wait_recv()
-        s1[to] = mine + near[to]
-        if d:
-            last.append(send(s1.at[to, :, pl.ds(0, 16)], a1.at[d], xs.at[d], xr.at[d], peer))
-    done = []
-    for d in (2, 1, 3):
-        to, peer = y_peer(d)
-        done.append(send(s1.at[:, to, pl.ds(16, 16)], b1.at[d], ys.at[d], yr.at[d], peer))
-    for copy in last:
-        copy.wait_recv()
-    s2a[...] = (s1[x, :, 0:16, :] + a1[1]) + (a1[2] + a1[3])
-    then = []
-    for d in (2, 1, 3):
-        to, peer = y_peer(d)
-        then.append(send(s2a.at[to], a2.at[d], y2s.at[d], y2r.at[d], peer))
-    for copy in done:
-        copy.wait_recv()
-    s2b[...] = (s1[:, y, 16:32, :] + b1[1]) + (b1[2] + b1[3])
-    for d in (2, 1, 3):
-        to, peer = x_peer(d)
-        then.append(send(s2b.at[to], b2.at[d], x2s.at[d], x2r.at[d], peer))
-    for copy in then[:3]:
-        copy.wait_recv()
-    low = (s2a[y] + a2[1]) + (a2[2] + a2[3])
-    for n in range(4):
-        s3[n] = low[n * 4 : (n + 1) * 4]
-    for copy in then[3:]:
-        copy.wait_recv()
-    high = (s2b[x] + b2[1]) + (b2[2] + b2[3])
-    for n in range(4):
-        s3[4 + n] = high[n * 4 : (n + 1) * 4]
+        total = total + near[to]
+        if dx == 0:
+            mine[...] = total
+        coded[to] = encode(total)
+        for dy in (2, 1, 3, 0):
+            if dx or dy:
+                to_x, to_y, peer = plane_peer(dx, dy)
+                at = coming.at[dx, dy]
+                then.append(send(coded.at[to_x, to_y], at, plane_s.at[dx, dy], plane_r.at[dx, dy], peer))
+    total = mine[y]
+    at = 0
+    for dx in order:
+        for dy in (2, 1, 3, 0):
+            if dx or dy:
+                then[at].wait_recv()
+                total = total + decode(coming[dx, dy])
+                at += 1
+    for n in range(8):
+        s3[n] = total[n * 4 : (n + 1) * 4]
     hear(2)
     third = []
     for d in (4, 3, 5, 2, 6, 1, 7):
@@ -346,7 +351,7 @@
         total = total + r3[d]
     data[...] = total[:, :256]
     weight[...] = total[:, 256:]
-    for copy in sends + to_near + last + done + then + third:
+    for copy in sends + to_near + then + third:
         copy.wait_send()
 
 
@@ -390,17 +395,12 @@
             dma((8,)), dma((8,)), dma((8,)), dma((8,)),
             VMEM((4, 4, 32, 384), F32),
             VMEM((4, 4, 32, 384), F32),
-            VMEM((4, 4, 32, 384), F32),
-            VMEM((4, 4, 16, 384), F32),
-            VMEM((4, 4, 16, 384), F32),
-            VMEM((4, 16, 384), F32),
-            VMEM((4, 16, 384), F32),
-            VMEM((4, 16, 384), F32),
-            VMEM((4, 16, 384), F32),
+            VMEM((4, 32, 384), F32),
+            VMEM((4, 4, 32, 384), jnp.int16),
+            VMEM((4, 4, 32, 384), jnp.int16),
             VMEM((8, 4, 384), F32),
             VMEM((8, 4, 384), F32),
-            dma((4,)), dma((4,)), dma((4,)), dma((4,)), dma((4,)), dma((4,)),
-            dma((4,)), dma((4,)), dma((4,)), dma((4,)), dma((8,)), dma((8,)),
+            dma((4,)), dma((4,)), dma((4, 4)), dma((4, 4)), dma((8,)), dma((8,)),
             pltpu.SemaphoreType.REGULAR((3, 2)),
         ],
         compiler_params=pltpu.CompilerParams(

time: 48.4 us -> 45.3 us (0.936)
  Pallas kernels: 44.9 us -> 41.9 us
    pallas_call x1, Pallas kernels: 44.9 us -> 41.9 us  [local(): pl.pallas_call(refine_kernel, out_shape=[jax.ShapeDtypeStruct((4, 256), F...]
where the time goes in v7:
time: 45.3 us; the launch traced here: 45.1 us
  Pallas kernels  41.9 us (92%)
  local copies, waits for them, and re-layouts  2.56 us (6%)
  between operations  0.65 us (1%)
    pallas_call x1, Pallas kernels, local(): pl.pallas_call(refine_kernel, out_shape=[jax.ShapeDtypeStruct((4, 256), F...  41.9 us
    unnamed x9, local copies, waits for them, and re-layouts  2.56 us

profile of v7, /device:TPU:1, one launch (start us, length us, event | category | flops | bytes accessed | tf_op | source)
XLA Modules:
  0.0 45.1 jit_solution(609258817797328588)
XLA Ops:
  0.6 41.9 %refine.1 = (f32[4,256]{1,0:T(4,128)}, f32[4,128]{1,0:T(4,128)}, f32[2,64]{1,0:T(2,128)}) custom-call(bf16[128,256]{1,0:T(8,128)(2,1)} %piece.1, bf16[2,2,2048]{2,1,0:T(2,128)(2,1)} %img_h.1, bf16[64,2048]{1,0:T(8,128)(2,1)} %ctf_h.1, s32[2]{0:T(128)} %cls_h.1, s32[32,4,64]{2,1,0:T(4,128)} %bitcast.6, s32[32,4,64]{2,1,0:T(4,128)} %bitcast.7, ...), custom_call_target="tpu_custom_call" | custom-call | tf_op jit(solution)/shard_map/refine/pallas_call | solution.py:363
  42.5 0.0 copy-start
  42.6 0.7 %copy-done = f32[4,256]{1,0:T(4,128)S(1)} copy-done((f32[4,256]{1,0:T(4,128)S(1)}, f32[4,256]{1,0:T(4,128)}, u32[]{:S(2)}) %copy-start) | copy-done | bytes 4120
  43.2 0.0 copy-start.1
  43.2 0.6 %copy.15 = f32[4,256]{1,0:T(4,128)} copy(f32[4,256]{1,0:T(4,128)S(1)} %copy-done) | data formatting | bytes 8192
  43.8 0.1 copy-done.1
  43.9 0.0 copy-start.2
  43.9 0.6 %copy.16 = f32[4,128]{1,0:T(4,128)} copy(f32[4,128]{1,0:T(4,128)S(1)} %copy-done.1) | data formatting | bytes 4096
  44.5 0.1 copy-done.2
  44.6 0.6 %copy.17 = f32[2,64]{1,0:T(2,128)} copy(f32[2,64]{1,0:T(2,128)S(1)} %copy-done.2) | data formatting | bytes 1024
Async XLA Ops:
  42.5 0.7 %copy-start = (f32[4,256]{1,0:T(4,128)S(1)}, f32[4,256]{1,0:T(4,128)}, u32[]{:S(2)}) copy-start(f32[4,256]{1,0:T(4,128)} %get-tuple-element.6) | copy-start | bytes 12292
  43.2 0.7 %copy-start.1 = (f32[4,128]{1,0:T(4,128)S(1)}, f32[4,128]{1,0:T(4,128)}, u32[]{:S(2)}) copy-start(f32[4,128]{1,0:T(4,128)} %get-tuple-element.7) | copy-start | bytes 6148
  43.9 0.7 %copy-start.2 = (f32[2,64]{1,0:T(2,128)S(1)}, f32[2,64]{1,0:T(2,128)}, u32[]{:S(2)}) copy-start(f32[2,64]{1,0:T(2,128)} %get-tuple-element.8) | copy-start | bytes 1540

commit v8 on v7

--- a/solution.py
+++ b/solution.py
@@ -19,8 +19,9 @@
 NBLK = 1024
 MESH = pl.DeviceIdType.MESH
 SLOTS = 4
-FLOOR = -34
-STEPS = 585
+OCTAVES = 44
+STEPS = 744
+LN2 = math.log(2.0)
 ORDER = (1, 2, 3, 4, 5, 6, 7)
 VMEM = pltpu.VMEM
 F32 = jnp.float32
@@ -61,14 +62,17 @@
 
 
 def encode(v):
-    size = jnp.log(jnp.maximum(jnp.abs(v), 2.0 ** (FLOOR - 1))) * (STEPS / math.log(2.0)) - FLOOR * STEPS
+    size = jnp.abs(v)
+    top = jnp.max(jnp.max(size, axis=0), axis=0, keepdims=True)
+    base = jnp.log(jnp.maximum(top, 1e-37)) - OCTAVES * LN2
+    size = (jnp.log(jnp.maximum(size, 1e-37)) - base) * (STEPS / LN2)
     size = jnp.maximum(size, 0.0) + 0.5
-    return jnp.where(v < 0, -size, size).astype(jnp.int32).astype(jnp.int16)
-
-
-def decode(code):
+    return jnp.where(v < 0, -size, size).astype(jnp.int32).astype(jnp.int16), base
+
+
+def decode(code, base):
     step = code.astype(jnp.int32).astype(F32)
-    size = jnp.exp(jnp.abs(step) * (math.log(2.0) / STEPS) + FLOOR * math.log(2.0))
+    size = jnp.exp(jnp.abs(step) * (LN2 / STEPS) + base)
     return jnp.where(step > 0, size, jnp.where(step < 0, -size, 0.0))
 
 
@@ -78,8 +82,8 @@
     img, ctf, cls, blk, kind, bank, fx, fy, own_sem,
     full, inter, table, parts, rows, rid_v, rids, rid_s, left, right,
     proj, cross, hist, gather_s, gather_r, forward_s, forward_r,
-    sums, near, mine, coded, coming, s3, r3,
-    near_s, near_r, plane_s, plane_r, zs, zr, here,
+    sums, near, mine, coded, coming, bases, their_bases, s3, r3,
+    near_s, near_r, plane_s, plane_r, base_s, base_r, zs, zr, here,
 ):
     p = lax.axis_index("particle")
     s = lax.axis_index("slab")
@@ -315,7 +319,7 @@
         to = lax.rem(x + d, 4)
         sums[to] = map_sums(1 - core, to)
         to_near.append(send(sums.at[to], near.at[to], near_s.at[n], near_r.at[n], sibling))
-    then = []
+    then, with_it = [], []
     for n, dx in enumerate(order):
         to = lax.rem(x + dx, 4)
         total = map_sums(core, to)
@@ -323,10 +327,12 @@
         total = total + near[to]
         if dx == 0:
             mine[...] = total
-        coded[to] = encode(total)
+        coded[to], bases[to] = encode(total)
         for dy in (2, 1, 3, 0):
             if dx or dy:
                 to_x, to_y, peer = plane_peer(dx, dy)
+                at = their_bases.at[dx, dy]
+                with_it.append(send(bases.at[to_x], at, base_s.at[dx, dy], base_r.at[dx, dy], peer))
                 at = coming.at[dx, dy]
                 then.append(send(coded.at[to_x, to_y], at, plane_s.at[dx, dy], plane_r.at[dx, dy], peer))
     total = mine[y]
@@ -334,8 +340,9 @@
     for dx in order:
         for dy in (2, 1, 3, 0):
             if dx or dy:
+                with_it[at].wait_recv()
                 then[at].wait_recv()
-                total = total + decode(coming[dx, dy])
+                total = total + decode(coming[dx, dy], their_bases[dx, dy])
                 at += 1
     for n in range(8):
         s3[n] = total[n * 4 : (n + 1) * 4]
@@ -351,7 +358,7 @@
         total = total + r3[d]
     data[...] = total[:, :256]
     weight[...] = total[:, 256:]
-    for copy in sends + to_near + then + third:
+    for copy in sends + to_near + then + with_it + third:
         copy.wait_send()
 
 
@@ -398,9 +405,12 @@
             VMEM((4, 32, 384), F32),
             VMEM((4, 4, 32, 384), jnp.int16),
             VMEM((4, 4, 32, 384), jnp.int16),
+            VMEM((4, 1, 384), F32),
+            VMEM((4, 4, 1, 384), F32),
             VMEM((8, 4, 384), F32),
             VMEM((8, 4, 384), F32),
-            dma((4,)), dma((4,)), dma((4, 4)), dma((4, 4)), dma((8,)), dma((8,)),
+            dma((4,)), dma((4,)), dma((4, 4)), dma((4, 4)), dma((4, 4)), dma((4, 4)),
+            dma((8,)), dma((8,)),
             pltpu.SemaphoreType.REGULAR((3, 2)),
         ],
         compiler_params=pltpu.CompilerParams(

time: 45.3 us -> 45.9 us (1.013)
  Pallas kernels: 41.9 us -> 42.5 us
    pallas_call x1, Pallas kernels: 41.9 us -> 42.5 us  [local(): pl.pallas_call(refine_kernel, out_shape=[jax.ShapeDtypeStruct((4, 256), F...]
where the time goes in v8:
time: 45.9 us; the launch traced here: 45.7 us
  Pallas kernels  42.5 us (93%)
  local copies, waits for them, and re-layouts  2.56 us (6%)
  between operations  0.65 us (1%)
    pallas_call x1, Pallas kernels, local(): pl.pallas_call(refine_kernel, out_shape=[jax.ShapeDtypeStruct((4, 256), F...  42.5 us
    unnamed x9, local copies, waits for them, and re-layouts  2.56 us

profile of v8, /device:TPU:1, one launch (start us, length us, event | category | flops | bytes accessed | tf_op | source)
XLA Modules:
  0.0 45.7 jit_solution(11605873526619826586)
XLA Ops:
  0.6 42.5 %refine.1 = (f32[4,256]{1,0:T(4,128)}, f32[4,128]{1,0:T(4,128)}, f32[2,64]{1,0:T(2,128)}) custom-call(bf16[128,256]{1,0:T(8,128)(2,1)} %piece.1, bf16[2,2,2048]{2,1,0:T(2,128)(2,1)} %img_h.1, bf16[64,2048]{1,0:T(8,128)(2,1)} %ctf_h.1, s32[2]{0:T(128)} %cls_h.1, s32[32,4,64]{2,1,0:T(4,128)} %bitcast.6, s32[32,4,64]{2,1,0:T(4,128)} %bitcast.7, ...), custom_call_target="tpu_custom_call" | custom-call | tf_op jit(solution)/shard_map/refine/pallas_call | solution.py:370
  43.1 0.0 copy-start
  43.2 0.7 %copy-done = f32[4,256]{1,0:T(4,128)S(1)} copy-done((f32[4,256]{1,0:T(4,128)S(1)}, f32[4,256]{1,0:T(4,128)}, u32[]{:S(2)}) %copy-start) | copy-done | bytes 4120
  43.8 0.0 copy-start.1
  43.8 0.6 %copy.15 = f32[4,256]{1,0:T(4,128)} copy(f32[4,256]{1,0:T(4,128)S(1)} %copy-done) | data formatting | bytes 8192
  44.4 0.1 copy-done.1
  44.5 0.0 copy-start.2
  44.5 0.6 %copy.16 = f32[4,128]{1,0:T(4,128)} copy(f32[4,128]{1,0:T(4,128)S(1)} %copy-done.1) | data formatting | bytes 4096
  45.1 0.1 copy-done.2
  45.1 0.6 %copy.17 = f32[2,64]{1,0:T(2,128)} copy(f32[2,64]{1,0:T(2,128)S(1)} %copy-done.2) | data formatting | bytes 1024
Async XLA Ops:
  43.1 0.7 %copy-start = (f32[4,256]{1,0:T(4,128)S(1)}, f32[4,256]{1,0:T(4,128)}, u32[]{:S(2)}) copy-start(f32[4,256]{1,0:T(4,128)} %get-tuple-element.6) | copy-start | bytes 12292
  43.8 0.7 %copy-start.1 = (f32[4,128]{1,0:T(4,128)S(1)}, f32[4,128]{1,0:T(4,128)}, u32[]{:S(2)}) copy-start(f32[4,128]{1,0:T(4,128)} %get-tuple-element.7) | copy-start | bytes 6148
  44.5 0.7 %copy-start.2 = (f32[2,64]{1,0:T(2,128)S(1)}, f32[2,64]{1,0:T(2,128)}, u32[]{:S(2)}) copy-start(f32[2,64]{1,0:T(2,128)} %get-tuple-element.8) | copy-start | bytes 1540

commit v9 on v8

--- a/solution.py
+++ b/solution.py
@@ -362,18 +362,31 @@
         copy.wait_send()
 
 
+def finish_kernel(data, weight, post, data_out, weight_out, post_out, sem):
+    copies = [
+        pltpu.make_async_copy(data, data_out, sem.at[0]),
+        pltpu.make_async_copy(weight, weight_out, sem.at[1]),
+        pltpu.make_async_copy(post, post_out, sem.at[2]),
+    ]
+    for copy in copies:
+        copy.start()
+    for copy in copies:
+        copy.wait()
+
+
 def local(ref_map, images, ctf_table, ctf_class, block_index, interp_kind, interp_bank):
     blk = jnp.transpose(block_index, (0, 2, 3, 1)).reshape(32, TAPS, CAND)
     kind = jnp.transpose(interp_kind, (0, 2, 3, 1)).reshape(32, TAPS, CAND)
     dma = pltpu.SemaphoreType.DMA
     i32 = jnp.int32
-    return pl.pallas_call(
+    shapes = [
+        jax.ShapeDtypeStruct((4, 256), F32),
+        jax.ShapeDtypeStruct((4, 128), F32),
+        jax.ShapeDtypeStruct((2, CAND), F32),
+    ]
+    results = pl.pallas_call(
         refine_kernel,
-        out_shape=[
-            jax.ShapeDtypeStruct((4, 256), F32),
-            jax.ShapeDtypeStruct((4, 128), F32),
-            jax.ShapeDtypeStruct((2, CAND), F32),
-        ],
+        out_shape=shapes,
         in_specs=[pl.BlockSpec(memory_space=pltpu.HBM)] * 9,
         out_specs=[pl.BlockSpec(memory_space=VMEM)] * 3,
         scratch_shapes=[
@@ -421,6 +434,15 @@
         ref_map, images, ctf_table, ctf_class, blk, kind, interp_bank,
         jnp.asarray(line_table(), BF16), jnp.asarray(across_table(), BF16),
     )
+    return pl.pallas_call(
+        finish_kernel,
+        out_shape=shapes,
+        in_specs=[pl.BlockSpec(memory_space=pltpu.HBM)] * 3,
+        out_specs=[pl.BlockSpec(memory_space=pltpu.HBM)] * 3,
+        scratch_shapes=[dma((3,))],
+        compiler_params=pltpu.CompilerParams(vmem_limit_bytes=56 * 1024 * 1024),
+        name="finish",
+    )(*results)
 
 
 def solution(mesh):

time: 45.9 us -> 44.6 us (0.972)
  local copies, waits for them, and re-layouts: 2.56 us -> 0 us
  Pallas kernels: 42.5 us -> 43.9 us
    unnamed x9 -> x0, local copies, waits for them, and re-layouts: 2.56 us -> none
    pallas_call x1 -> x2, Pallas kernels: 42.5 us -> 43.9 us  [the longest x1 42.5 us: local(): pl.pallas_call(refine_kernel, out_shape=shapes, in_specs=[pl.BlockSpec(me...]
where the time goes in v9:
time: 44.6 us; the launch traced here: 44.5 us
  Pallas kernels  43.9 us (98%)
  between operations  0.64 us (1%)
    pallas_call x1, Pallas kernels, local(): pl.pallas_call(refine_kernel, out_shape=shapes, in_specs=[pl.BlockSpec(me...  42.5 us
    pallas_call x1, Pallas kernels, local(): pl.pallas_call(finish_kernel, out_shape=shapes, in_specs=[pl.BlockSpec(me...  1.35 us

profile of v9, /device:TPU:1, one launch (start us, length us, event | category | flops | bytes accessed | tf_op | source)
XLA Modules:
  0.0 44.5 jit_solution(17654293744216548780)
XLA Ops:
  0.6 42.5 %refine.1 = (f32[4,256]{1,0:T(4,128)}, f32[4,128]{1,0:T(4,128)}, f32[2,64]{1,0:T(2,128)}) custom-call(bf16[128,256]{1,0:T(8,128)(2,1)} %piece.1, bf16[2,2,2048]{2,1,0:T(2,128)(2,1)} %img_h.1, bf16[64,2048]{1,0:T(8,128)(2,1)} %ctf_h.1, s32[2]{0:T(128)} %cls_h.1, s32[32,4,64]{2,1,0:T(4,128)} %bitcast.6, s32[32,4,64]{2,1,0:T(4,128)} %bitcast.7, ...), custom_call_target="tpu_custom_call" | custom-call | tf_op jit(solution)/shard_map/refine/pallas_call | solution.py:387
  43.1 1.3 %finish.1 = (f32[4,256]{1,0:T(4,128)}, f32[4,128]{1,0:T(4,128)}, f32[2,64]{1,0:T(2,128)}) custom-call(f32[4,256]{1,0:T(4,128)} %get-tuple-element.6.data, f32[4,128]{1,0:T(4,128)} %get-tuple-element.7.weight, f32[2,64]{1,0:T(2,128)} %get-tuple-element.8.post), custom_call_target="tpu_custom_call" | custom-call | tf_op jit(solution)/shard_map/finish/pallas_call | solution.py:437

commit v10 on v9

--- a/solution.py
+++ b/solution.py
@@ -22,7 +22,7 @@
 OCTAVES = 44
 STEPS = 744
 LN2 = math.log(2.0)
-ORDER = (1, 2, 3, 4, 5, 6, 7)
+ORDER = (5, 4, 3, 2, 7, 6, 1)
 VMEM = pltpu.VMEM
 F32 = jnp.float32
 BF16 = jnp.bfloat16
@@ -224,12 +224,15 @@
         forward(n, other_half).wait_recv()
         map_piece(map_peer(n, -1)[1])
 
-    pass_on(1)
+    def nth(k):
+        return lax.rem(2 * k - 1, 7) + 1
+
+    pass_on(2)
 
     @pl.loop(1, 7)
-    def _(n):
-        pass_on(n + 1)
-        use(n)
+    def _(k):
+        pass_on(nth(k + 1))
+        use(nth(k))
 
     use(7)
     for n in range(1, 8):

time: 44.6 us -> 44.9 us (level)
  no operation moved by 1% of the time
where the time goes in v10:
time: 44.9 us; the launch traced here: 44.8 us
  Pallas kernels  44.1 us (98%)
  between operations  0.64 us (1%)
    pallas_call x1, Pallas kernels, local(): pl.pallas_call(refine_kernel, out_shape=shapes, in_specs=[pl.BlockSpec(me...  42.8 us
    pallas_call x1, Pallas kernels, local(): pl.pallas_call(finish_kernel, out_shape=shapes, in_specs=[pl.BlockSpec(me...  1.35 us

profile of v10, /device:TPU:1, one launch (start us, length us, event | category | flops | bytes accessed | tf_op | source)
XLA Modules:
  0.0 44.8 jit_solution(18222218476579204)
XLA Ops:
  0.6 42.8 %refine.1 = (f32[4,256]{1,0:T(4,128)}, f32[4,128]{1,0:T(4,128)}, f32[2,64]{1,0:T(2,128)}) custom-call(bf16[128,256]{1,0:T(8,128)(2,1)} %piece.1, bf16[2,2,2048]{2,1,0:T(2,128)(2,1)} %img_h.1, bf16[64,2048]{1,0:T(8,128)(2,1)} %ctf_h.1, s32[2]{0:T(128)} %cls_h.1, s32[32,4,64]{2,1,0:T(4,128)} %bitcast.6, s32[32,4,64]{2,1,0:T(4,128)} %bitcast.7, ...), custom_call_target="tpu_custom_call" | custom-call | tf_op jit(solution)/shard_map/refine/pallas_call | solution.py:390
  43.4 1.3 %finish.1 = (f32[4,256]{1,0:T(4,128)}, f32[4,128]{1,0:T(4,128)}, f32[2,64]{1,0:T(2,128)}) custom-call(f32[4,256]{1,0:T(4,128)} %get-tuple-element.6.data, f32[4,128]{1,0:T(4,128)} %get-tuple-element.7.weight, f32[2,64]{1,0:T(2,128)} %get-tuple-element.8.post), custom_call_target="tpu_custom_call" | custom-call | tf_op jit(solution)/shard_map/finish/pallas_call | solution.py:440

commit v11 on v9

--- a/solution.py
+++ b/solution.py
@@ -117,8 +117,8 @@
         copy.start()
         return copy
 
-    peers = [sibling] + [x_peer(d)[1] for d in (1, 2, 3)] + [z_peer(d)[1] for d in (1, 7)]
-    peers += [map_peer(n, 1) for n in range(1, 8)]
+    peers = [map_peer(n, 1) for n in (5, 3, 7, 4)] + [x_peer(d)[1] for d in (2, 1, 3)]
+    peers += [map_peer(n, 1) for n in (1, 2, 6)] + [z_peer(d)[1] for d in (1, 7)] + [sibling]
     barrier = pltpu.get_barrier_semaphore()
     for peer in peers:
         pl.semaphore_signal(barrier, inc=1, device_id=peer, device_id_type=MESH)

time: 44.6 us -> 44.5 us (level)
  no operation moved by 1% of the time
where the time goes in v11:
time: 44.5 us; the launch traced here: 44.4 us
  Pallas kernels  43.8 us (98%)
  between operations  0.64 us (1%)
    pallas_call x1, Pallas kernels, local(): pl.pallas_call(refine_kernel, out_shape=shapes, in_specs=[pl.BlockSpec(me...  42.4 us
    pallas_call x1, Pallas kernels, local(): pl.pallas_call(finish_kernel, out_shape=shapes, in_specs=[pl.BlockSpec(me...  1.35 us

profile of v11, /device:TPU:1, one launch (start us, length us, event | category | flops | bytes accessed | tf_op | source)
XLA Modules:
  0.0 44.4 jit_solution(15731023480614592284)
XLA Ops:
  0.6 42.4 %refine.1 = (f32[4,256]{1,0:T(4,128)}, f32[4,128]{1,0:T(4,128)}, f32[2,64]{1,0:T(2,128)}) custom-call(bf16[128,256]{1,0:T(8,128)(2,1)} %piece.1, bf16[2,2,2048]{2,1,0:T(2,128)(2,1)} %img_h.1, bf16[64,2048]{1,0:T(8,128)(2,1)} %ctf_h.1, s32[2]{0:T(128)} %cls_h.1, s32[32,4,64]{2,1,0:T(4,128)} %bitcast.6, s32[32,4,64]{2,1,0:T(4,128)} %bitcast.7, ...), custom_call_target="tpu_custom_call" | custom-call | tf_op jit(solution)/shard_map/refine/pallas_call | solution.py:387
  43.1 1.3 %finish.1 = (f32[4,256]{1,0:T(4,128)}, f32[4,128]{1,0:T(4,128)}, f32[2,64]{1,0:T(2,128)}) custom-call(f32[4,256]{1,0:T(4,128)} %get-tuple-element.6.data, f32[4,128]{1,0:T(4,128)} %get-tuple-element.7.weight, f32[2,64]{1,0:T(2,128)} %get-tuple-element.8.post), custom_call_target="tpu_custom_call" | custom-call | tf_op jit(solution)/shard_map/finish/pallas_call | solution.py:437

commit v12 on v11

--- a/solution.py
+++ b/solution.py
@@ -232,9 +232,6 @@
         use(n)
 
     use(7)
-    for n in range(1, 8):
-        forward(n, half).wait_send()
-
     hear(0)
     tell(1)
     loads[7].wait()
@@ -358,6 +355,8 @@
         total = total + r3[d]
     data[...] = total[:, :256]
     weight[...] = total[:, 256:]
+    for n in range(1, 8):
+        forward(n, half).wait_send()
     for copy in sends + to_near + then + with_it + third:
         copy.wait_send()
 

time: 44.5 us -> 44.5 us (level)
  no operation moved by 1% of the time
where the time goes in v12:
time: 44.5 us; the launch traced here: 44.4 us
  Pallas kernels  43.8 us (98%)
  between operations  0.64 us (1%)
    pallas_call x1, Pallas kernels, local(): pl.pallas_call(refine_kernel, out_shape=shapes, in_specs=[pl.BlockSpec(me...  42.4 us
    pallas_call x1, Pallas kernels, local(): pl.pallas_call(finish_kernel, out_shape=shapes, in_specs=[pl.BlockSpec(me...  1.35 us

profile of v12, /device:TPU:1, one launch (start us, length us, event | category | flops | bytes accessed | tf_op | source)
XLA Modules:
  0.0 44.4 jit_solution(11292987871856654980)
XLA Ops:
  0.6 42.4 %refine.1 = (f32[4,256]{1,0:T(4,128)}, f32[4,128]{1,0:T(4,128)}, f32[2,64]{1,0:T(2,128)}) custom-call(bf16[128,256]{1,0:T(8,128)(2,1)} %piece.1, bf16[2,2,2048]{2,1,0:T(2,128)(2,1)} %img_h.1, bf16[64,2048]{1,0:T(8,128)(2,1)} %ctf_h.1, s32[2]{0:T(128)} %cls_h.1, s32[32,4,64]{2,1,0:T(4,128)} %bitcast.6, s32[32,4,64]{2,1,0:T(4,128)} %bitcast.7, ...), custom_call_target="tpu_custom_call" | custom-call | tf_op jit(solution)/shard_map/refine/pallas_call | solution.py:386
  43.1 1.3 %finish.1 = (f32[4,256]{1,0:T(4,128)}, f32[4,128]{1,0:T(4,128)}, f32[2,64]{1,0:T(2,128)}) custom-call(f32[4,256]{1,0:T(4,128)} %get-tuple-element.6.data, f32[4,128]{1,0:T(4,128)} %get-tuple-element.7.weight, f32[2,64]{1,0:T(2,128)} %get-tuple-element.8.post), custom_call_target="tpu_custom_call" | custom-call | tf_op jit(solution)/shard_map/finish/pallas_call | solution.py:436

commit v13 on v11

--- a/solution.py
+++ b/solution.py
@@ -299,7 +299,7 @@
     for i in range(2):
         pair = split(jnp.concatenate([weights[i], weights[i]], axis=1))
 
-        @pl.loop(0, PB, unroll=8)
+        @pl.loop(0, PB, unroll=PB)
         def _(b):
             histogram(i, b, *pair)
 

time: 44.5 us -> 44 us (0.989)
  Pallas kernels: 43.8 us -> 43.3 us
    pallas_call x1, Pallas kernels: 42.4 us -> 41.9 us  [local(): pl.pallas_call(refine_kernel, out_shape=shapes, in_specs=[pl.BlockSpec(me...]
where the time goes in v13:
time: 44 us; the launch traced here: 43.9 us
  Pallas kernels  43.3 us (98%)
  between operations  0.64 us (1%)
    pallas_call x1, Pallas kernels, local(): pl.pallas_call(refine_kernel, out_shape=shapes, in_specs=[pl.BlockSpec(me...  41.9 us
    pallas_call x1, Pallas kernels, local(): pl.pallas_call(finish_kernel, out_shape=shapes, in_specs=[pl.BlockSpec(me...  1.35 us

profile of v13, /device:TPU:1, one launch (start us, length us, event | category | flops | bytes accessed | tf_op | source)
XLA Modules:
  0.0 43.9 jit_solution(16895340281742413614)
XLA Ops:
  0.6 41.9 %refine.1 = (f32[4,256]{1,0:T(4,128)}, f32[4,128]{1,0:T(4,128)}, f32[2,64]{1,0:T(2,128)}) custom-call(bf16[128,256]{1,0:T(8,128)(2,1)} %piece.1, bf16[2,2,2048]{2,1,0:T(2,128)(2,1)} %img_h.1, bf16[64,2048]{1,0:T(8,128)(2,1)} %ctf_h.1, s32[2]{0:T(128)} %cls_h.1, s32[32,4,64]{2,1,0:T(4,128)} %bitcast.6, s32[32,4,64]{2,1,0:T(4,128)} %bitcast.7, ...), custom_call_target="tpu_custom_call" | custom-call | tf_op jit(solution)/shard_map/refine/pallas_call | solution.py:387
  42.6 1.3 %finish.1 = (f32[4,256]{1,0:T(4,128)}, f32[4,128]{1,0:T(4,128)}, f32[2,64]{1,0:T(2,128)}) custom-call(f32[4,256]{1,0:T(4,128)} %get-tuple-element.6.data, f32[4,128]{1,0:T(4,128)} %get-tuple-element.7.weight, f32[2,64]{1,0:T(2,128)} %get-tuple-element.8.post), custom_call_target="tpu_custom_call" | custom-call | tf_op jit(solution)/shard_map/finish/pallas_call | solution.py:437
